TPU v7x, 128 devices: a whole 4x4x4 slice. The times are simulated.
128 devices in a mesh: section: 2 (over z_lo), dp: 16 (over y, x), ctx: 4 (over z_hi, core).
Axes of the slice: x: 4, y: 4, z: 4 (z_hi: 2, z_lo: 2; z = z_hi * 2 + z_lo), core: 2. Of those that a mesh axis runs over, the one named last changes fastest.
Arguments:
- ends_in: bfloat16 [2, 2, 16, 512, 896], P('section', None, 'dp', 'ctx'), may hold values from -6 to 6
- segment_ids: int32 [2, 16, 512], P(None, 'dp', 'ctx'), may hold values from 0 to 3, as said below
- norm_gains: bfloat16 [2, 2, 896], P('section', None, ('dp', 'ctx')), may hold values from 0.25 to 1.75
- qkv_weight: bfloat16 [2, 896, 1152], P('section', ('dp', 'ctx')), may hold values from -1.6035675 to 1.6035675
- qkv_bias: bfloat16 [2, 1152], P('section', ('dp', 'ctx')), may hold values from -3 to 3
- out_weight: bfloat16 [2, 896, 896], P('section', ('dp', 'ctx')), may hold values from -0.1875 to 0.1875
- in_weight: bfloat16 [2, 896, 9728], P('section', ('dp', 'ctx')), may hold values from -0.1875 to 0.1875
- down_weight: bfloat16 [2, 4864, 896], P('section', ('dp', 'ctx')), may hold values from -0.15625 to 0.15625
Outputs:
- ends_out: float32 [2, 2, 16, 512, 896], P('section', None, 'dp', 'ctx')
- grad_gains: float32 [2, 2, 896], P('section', None, ('dp', 'ctx'))
- grad_qkv_weight: float32 [2, 896, 1152], P('section', ('dp', 'ctx'))
- grad_qkv_bias: float32 [2, 1152], P('section', ('dp', 'ctx'))
- grad_out_weight: float32 [2, 896, 896], P('section', ('dp', 'ctx'))
- grad_in_weight: float32 [2, 896, 9728], P('section', ('dp', 'ctx'))
- grad_down_weight: float32 [2, 4864, 896], P('section', ('dp', 'ctx'))
Inputs may be any that keep to these rules, and one draw needn't show every extreme that they name: `segment_ids`: in every pack the ids start at 0 and never fall along the positions. Among the 2 x 1 packs that share an index of dp, one holds a document that begins within the first 128 positions and ends within the last 128.
All inputs are finite; a program needn't handle non-finite values.
Results may differ from a plain program's by a relative error of at most 0.03.
Values may be sent and summed in bfloat16 or wider, within the bound.
A program may use at most 192 MiB of HBM per device.

v0:
```python
import jax
import jax.numpy as jnp
from jax import lax
from jax.sharding import PartitionSpec as P

HEADS = 14
KV_HEADS = 2
HEAD = 64
FF = 4864


epsilon = 1e-06
rope_base = 1000000.0
masked_score = -1000000000.0


def from_behind(value, axis, steps):
    count = lax.axis_size(axis)
    initial, last = (max(0, -steps), min(count, count - steps))
    return lax.ppermute(value, axis, [(source, source + steps) for source in range(initial, last)])


def rms_scale(residual, gain_row):
    return (
        residual
        * lax.rsqrt(jnp.mean(residual * residual, axis=-1, keepdims=True) + epsilon)
        * gain_row
    )


def rotate(tensor, rope_cos, rope_sin):
    half_dim = tensor.shape[-1] // 2
    turned = jnp.concatenate([-tensor[..., half_dim:], tensor[..., :half_dim]], axis=-1)
    return tensor * rope_cos + turned * rope_sin


def unrotate(tensor, rope_cos, rope_sin):
    half_dim = tensor.shape[-1] // 2
    scaled = tensor * rope_sin
    turned = jnp.concatenate([scaled[..., half_dim:], -scaled[..., :half_dim]], axis=-1)
    return tensor * rope_cos + turned


def take_slot(buffer, slot_idx):
    return lax.dynamic_index_in_dim(buffer, slot_idx, 0, keepdims=False)


def put_slot(buffer, new_value, slot_idx, active):
    return lax.dynamic_update_index_in_dim(
        buffer, jnp.where(active, new_value, take_slot(buffer, slot_idx)), slot_idx, 0
    )


def project(residual, rope_cos, rope_sin, params):
    leading = residual.shape[:2]
    q_width = HEADS * HEAD
    kv_width = KV_HEADS * HEAD
    normed = rms_scale(residual, params[0][0].astype(jnp.float32)).astype(jnp.bfloat16)
    linear = jnp.dot(normed, params[1], preferred_element_type=jnp.float32) + params[2].astype(
        jnp.float32
    )
    queries = rotate(
        linear[..., :q_width].reshape(leading + (HEADS, HEAD)), rope_cos, rope_sin
    ) * HEAD ** (-0.5)
    key_rows = rotate(
        linear[..., q_width : q_width + kv_width].reshape(leading + (KV_HEADS, HEAD)),
        rope_cos,
        rope_sin,
    )
    value_rows = linear[..., q_width + kv_width :]
    return (
        queries.reshape(leading + (q_width,)).astype(jnp.bfloat16),
        key_rows.reshape(leading + (kv_width,)).astype(jnp.bfloat16),
        value_rows.astype(jnp.bfloat16),
    )


def project_skip(residual, rope_cos, rope_sin, params):
    leading = residual.shape[:2]
    return (
        jnp.zeros(leading + (HEADS * HEAD,), jnp.bfloat16),
        jnp.zeros(leading + (KV_HEADS * HEAD,), jnp.bfloat16),
        jnp.zeros(leading + (KV_HEADS * HEAD,), jnp.bfloat16),
    )


def attention_scores(queries, key_all, allowed):
    leading = queries.shape[:2]
    q_heads = queries.reshape(leading + (KV_HEADS, HEADS // KV_HEADS, HEAD))
    k_heads = key_all.reshape(key_all.shape[:2] + (KV_HEADS, HEAD))
    scores = jnp.einsum("sqgja,skga->sgjqk", q_heads, k_heads, preferred_element_type=jnp.float32)
    return (jnp.where(allowed[:, None, None], scores, masked_score), q_heads, k_heads)


def forward_tail(residual, queries, key_all, value_all, allowed, params):
    scores, q_heads, k_heads = attention_scores(queries, key_all, allowed)
    top_score = jnp.max(scores, axis=-1, keepdims=True)
    exp_scores = jnp.exp(scores - top_score)
    exp_total = jnp.sum(exp_scores, axis=-1, keepdims=True)
    attn_probs = (exp_scores / exp_total).astype(jnp.bfloat16)
    v_heads = value_all.reshape(value_all.shape[:2] + (KV_HEADS, HEAD))
    attended = jnp.einsum(
        "sgjqk,skga->sqgja", attn_probs, v_heads, preferred_element_type=jnp.float32
    )
    attended = attended.reshape(residual.shape[:2] + (HEADS * HEAD,)).astype(jnp.bfloat16)
    middle = residual + jnp.dot(attended, params[3], preferred_element_type=jnp.float32)
    normed = rms_scale(middle, params[0][1].astype(jnp.float32)).astype(jnp.bfloat16)
    gate_up = jnp.dot(normed, params[4], preferred_element_type=jnp.float32)
    hidden = (jax.nn.silu(gate_up[..., :FF]) * gate_up[..., FF:]).astype(jnp.bfloat16)
    result = middle + jnp.dot(hidden, params[5], preferred_element_type=jnp.float32)
    return (result, middle, gate_up, attended, (top_score + jnp.log(exp_total))[..., 0])


def tail_skip(residual, queries, key_all, value_all, allowed, params):
    leading = residual.shape[:2]
    return (
        jnp.zeros(residual.shape, jnp.float32),
        jnp.zeros(residual.shape, jnp.float32),
        jnp.zeros(leading + (2 * FF,), jnp.float32),
        jnp.zeros(leading + (HEADS * HEAD,), jnp.bfloat16),
        jnp.zeros((leading[0], KV_HEADS, HEADS // KV_HEADS, leading[1]), jnp.float32),
    )


def tail_backward(
    grad_out, middle, gate_up, attended, queries, log_total, key_all, value_all, allowed, params
):
    leading = grad_out.shape[:2]
    grad_low = grad_out.astype(jnp.bfloat16)
    gate_part = gate_up[..., :FF]
    up_part = gate_up[..., FF:]
    sigmoid_gate = jax.nn.sigmoid(gate_part)
    silu_gate = jax.nn.silu(gate_part)
    hidden = (silu_gate * up_part).astype(jnp.bfloat16)
    grad_hidden = jnp.einsum("scd,fd->scf", grad_low, params[5], preferred_element_type=jnp.float32)
    grad_gate = grad_hidden * up_part * sigmoid_gate * (1.0 + gate_part * (1.0 - sigmoid_gate))
    grad_gu = jnp.concatenate([grad_gate, grad_hidden * silu_gate], axis=-1).astype(jnp.bfloat16)
    normed, norm_pull = jax.vjp(rms_scale, middle, params[0][1].astype(jnp.float32))
    grad_normed = jnp.einsum("scf,df->scd", grad_gu, params[4], preferred_element_type=jnp.float32)
    grad_mid_norm, grad_gain_b = norm_pull(grad_normed)
    grad_middle = grad_out + grad_mid_norm
    grad_branch = grad_middle.astype(jnp.bfloat16)
    grad_att = jnp.einsum(
        "scd,ed->sce", grad_branch, params[3], preferred_element_type=jnp.float32
    ).astype(jnp.bfloat16)
    scores, q_heads, k_heads = attention_scores(queries, key_all, allowed)
    attn_probs = jnp.exp(scores - log_total[..., None])
    v_heads = value_all.reshape(value_all.shape[:2] + (KV_HEADS, HEAD))
    g_heads = grad_att.reshape(leading + (KV_HEADS, HEADS // KV_HEADS, HEAD))
    grad_probs = jnp.einsum(
        "sqgja,skga->sgjqk", g_heads, v_heads, preferred_element_type=jnp.float32
    )
    grad_values = jnp.einsum(
        "sgjqk,sqgja->skga",
        attn_probs.astype(jnp.bfloat16),
        g_heads,
        preferred_element_type=jnp.float32,
    )
    inner_sum = jnp.sum(attn_probs * grad_probs, axis=-1, keepdims=True)
    grad_scores = (attn_probs * (grad_probs - inner_sum)).astype(jnp.bfloat16)
    grad_queries = jnp.einsum(
        "sgjqk,skga->sqgja", grad_scores, k_heads, preferred_element_type=jnp.float32
    )
    grad_keys = jnp.einsum(
        "sgjqk,sqgja->skga", grad_scores, q_heads, preferred_element_type=jnp.float32
    )
    pieces = (attended, grad_branch, normed.astype(jnp.bfloat16), grad_gu, hidden, grad_low)
    return (
        grad_queries.reshape(queries.shape),
        grad_keys.reshape(key_all.shape),
        grad_values.reshape(key_all.shape),
        grad_middle,
        grad_gain_b,
        pieces,
    )


def tail_back_skip(
    grad_out, middle, gate_up, attended, queries, log_total, key_all, value_all, allowed, params
):
    leading = grad_out.shape[:2]
    pieces = (
        jnp.zeros(attended.shape, jnp.bfloat16),
        jnp.zeros(grad_out.shape, jnp.bfloat16),
        jnp.zeros(grad_out.shape, jnp.bfloat16),
        jnp.zeros(leading + (2 * FF,), jnp.bfloat16),
        jnp.zeros(leading + (FF,), jnp.bfloat16),
        jnp.zeros(grad_out.shape, jnp.bfloat16),
    )
    return (
        jnp.zeros(queries.shape, jnp.float32),
        jnp.zeros(key_all.shape, jnp.float32),
        jnp.zeros(key_all.shape, jnp.float32),
        jnp.zeros(grad_out.shape, jnp.float32),
        jnp.zeros((grad_out.shape[-1],), jnp.float32),
        pieces,
    )


def head_backward(
    grad_queries, grad_keys, grad_values, grad_middle, residual, rope_cos, rope_sin, params
):
    leading = residual.shape[:2]
    grad_q_lin = unrotate(
        grad_queries.reshape(leading + (HEADS, HEAD)) * HEAD ** (-0.5), rope_cos, rope_sin
    )
    grad_k_lin = unrotate(grad_keys.reshape(leading + (KV_HEADS, HEAD)), rope_cos, rope_sin)
    grad_linear = jnp.concatenate(
        [
            grad_q_lin.reshape(leading + (HEADS * HEAD,)),
            grad_k_lin.reshape(leading + (KV_HEADS * HEAD,)),
            grad_values,
        ],
        axis=-1,
    ).astype(jnp.bfloat16)
    normed, norm_pull = jax.vjp(rms_scale, residual, params[0][0].astype(jnp.float32))
    grad_normed = jnp.einsum(
        "sce,de->scd", grad_linear, params[1], preferred_element_type=jnp.float32
    )
    grad_in_norm, grad_gain_a = norm_pull(grad_normed)
    grad_bias = jnp.sum(grad_linear.astype(jnp.float32), axis=(0, 1))
    return (
        grad_middle + grad_in_norm,
        grad_gain_a,
        grad_bias,
        (normed.astype(jnp.bfloat16), grad_linear),
    )


def head_skip(
    grad_queries, grad_keys, grad_values, grad_middle, residual, rope_cos, rope_sin, params
):
    leading = residual.shape[:2]
    return (
        jnp.zeros(residual.shape, jnp.float32),
        jnp.zeros((residual.shape[-1],), jnp.float32),
        jnp.zeros((params[2].shape[0],), jnp.float32),
        (
            jnp.zeros(residual.shape, jnp.bfloat16),
            jnp.zeros(leading + (params[1].shape[1],), jnp.bfloat16),
        ),
    )


def contract_rows(left_rows, right_rows):
    left_flat = left_rows.reshape(-1, left_rows.shape[-1])
    right_flat = right_rows.reshape(-1, right_rows.shape[-1])
    return lax.dot_general(
        left_flat, right_flat, (((0,), (0,)), ((), ())), preferred_element_type=jnp.float32
    )


def weight_grads(gain_sums, bias_sums, pieces):
    normed_a, grad_linear, attended, grad_branch, normed_b, grad_gu, hidden, grad_low = pieces
    return (
        gain_sums,
        contract_rows(normed_a, grad_linear),
        bias_sums,
        contract_rows(attended, grad_branch),
        contract_rows(normed_b, grad_gu),
        contract_rows(hidden, grad_low),
    )


def per_device(
    ends_in, segment_ids, norm_gains, qkv_weight, qkv_bias, out_weight, in_weight, down_weight
):
    section_idx = lax.axis_index("section")
    section_count = lax.axis_size("section")
    micro_count = ends_in.shape[1]
    seq_here = ends_in.shape[2]
    shard_len = ends_in.shape[3]
    width_model = ends_in.shape[4]
    tick_count = micro_count + section_count - 1
    pack_ids = lax.all_gather(segment_ids, "ctx", axis=2, tiled=True)
    full_len = pack_ids.shape[2]
    indices = jnp.arange(full_len, dtype=jnp.int32)
    starts_here = jnp.concatenate(
        [jnp.ones(pack_ids.shape[:2] + (1,), dtype=bool), pack_ids[..., 1:] != pack_ids[..., :-1]],
        axis=-1,
    )
    doc_start = lax.cummax(jnp.where(starts_here, indices, 0), axis=2)
    offset = lax.axis_index("ctx") * shard_len
    own_pos = lax.dynamic_slice_in_dim(indices - doc_start, offset, shard_len, 2).astype(
        jnp.float32
    )
    own_ids = lax.dynamic_slice_in_dim(pack_ids, offset, shard_len, 2)
    own_index = offset + jnp.arange(shard_len, dtype=jnp.int32)
    allowed = (own_ids[..., :, None] == pack_ids[..., None, :]) & (
        indices[None, :] <= own_index[:, None]
    )
    frequency = rope_base ** (-jnp.arange(0, HEAD, 2, dtype=jnp.float32) / HEAD)
    angles = own_pos[..., None] * frequency
    rope_cos = jnp.concatenate([jnp.cos(angles), jnp.cos(angles)], axis=-1)[..., None, :]
    rope_sin = jnp.concatenate([jnp.sin(angles), jnp.sin(angles)], axis=-1)[..., None, :]
    full_fwd = (
        lax.all_gather(norm_gains[0], ("dp", "ctx"), axis=1, tiled=True),
        lax.all_gather(qkv_weight[0], ("dp", "ctx"), axis=0, tiled=True),
        lax.all_gather(qkv_bias[0], ("dp", "ctx"), axis=0, tiled=True),
        lax.all_gather(out_weight[0], ("dp", "ctx"), axis=0, tiled=True),
        lax.all_gather(in_weight[0], ("dp", "ctx"), axis=0, tiled=True),
        lax.all_gather(down_weight[0], ("dp", "ctx"), axis=0, tiled=True),
    )

    def empty_keep(last_dim, elem_type):
        return jnp.zeros((micro_count, seq_here, shard_len, last_dim), elem_type)

    kv_width = KV_HEADS * HEAD
    keep_residual = empty_keep(width_model, jnp.float32)
    keep_queries = empty_keep(HEADS * HEAD, jnp.bfloat16)
    keep_keys = empty_keep(kv_width, jnp.bfloat16)
    keep_values = empty_keep(kv_width, jnp.bfloat16)
    keep_attended = empty_keep(HEADS * HEAD, jnp.bfloat16)
    keep_middle = empty_keep(width_model, jnp.float32)
    keep_gate_up = empty_keep(2 * FF, jnp.float32)
    keep_lse = jnp.zeros(
        (micro_count, seq_here, KV_HEADS, HEADS // KV_HEADS, shard_len), jnp.float32
    )
    results = empty_keep(width_model, jnp.float32)
    incoming = jnp.zeros((seq_here, shard_len, width_model), jnp.bfloat16)
    for tick_idx in range(tick_count):
        slot_raw = tick_idx - section_idx
        active = (slot_raw >= 0) & (slot_raw < micro_count)
        slot_idx = jnp.clip(slot_raw, 0, micro_count - 1)
        residual = jnp.where(
            section_idx == 0, ends_in[0, min(tick_idx, micro_count - 1)], incoming
        ).astype(jnp.float32)
        cos_here = take_slot(rope_cos, slot_idx)
        sin_here = take_slot(rope_sin, slot_idx)
        mask_here = take_slot(allowed, slot_idx)
        queries, key_rows, value_rows = lax.cond(
            active, project, project_skip, residual, cos_here, sin_here, full_fwd
        )
        key_all, value_all = (
            lax.all_gather(key_rows, "ctx", axis=1, tiled=True),
            lax.all_gather(value_rows, "ctx", axis=1, tiled=True),
        )
        result, middle, gate_up, attended, log_total = lax.cond(
            active,
            forward_tail,
            tail_skip,
            residual,
            queries,
            key_all,
            value_all,
            mask_here,
            full_fwd,
        )
        if tick_idx + 1 < tick_count:
            incoming = from_behind(result.astype(jnp.bfloat16), "section", 1)
        keep_residual = put_slot(keep_residual, residual, slot_idx, active)
        keep_queries = put_slot(keep_queries, queries, slot_idx, active)
        keep_keys = put_slot(keep_keys, key_rows, slot_idx, active)
        keep_values = put_slot(keep_values, value_rows, slot_idx, active)
        keep_attended = put_slot(keep_attended, attended, slot_idx, active)
        keep_middle = put_slot(keep_middle, middle, slot_idx, active)
        keep_gate_up = put_slot(keep_gate_up, gate_up, slot_idx, active)
        keep_lse = put_slot(keep_lse, log_total, slot_idx, active)
        results = put_slot(results, result, slot_idx, active & (section_idx == section_count - 1))
    full_bwd = (
        lax.all_gather(norm_gains[0], ("dp", "ctx"), axis=1, tiled=True),
        lax.all_gather(qkv_weight[0], ("dp", "ctx"), axis=0, tiled=True),
        lax.all_gather(qkv_bias[0], ("dp", "ctx"), axis=0, tiled=True),
        lax.all_gather(out_weight[0], ("dp", "ctx"), axis=0, tiled=True),
        lax.all_gather(in_weight[0], ("dp", "ctx"), axis=0, tiled=True),
        lax.all_gather(down_weight[0], ("dp", "ctx"), axis=0, tiled=True),
    )
    keep_pieces = (
        empty_keep(width_model, jnp.bfloat16),
        empty_keep(full_bwd[1].shape[1], jnp.bfloat16),
        empty_keep(HEADS * HEAD, jnp.bfloat16),
        empty_keep(width_model, jnp.bfloat16),
        empty_keep(width_model, jnp.bfloat16),
        empty_keep(2 * FF, jnp.bfloat16),
        empty_keep(FF, jnp.bfloat16),
        empty_keep(width_model, jnp.bfloat16),
    )
    gain_sums = jnp.zeros((2, width_model), jnp.float32)
    bias_sums = jnp.zeros((full_bwd[1].shape[1],), jnp.float32)
    shard_sums = ()
    incoming_grad = jnp.zeros((seq_here, shard_len, width_model), jnp.bfloat16)
    for tick_idx in range(tick_count):
        slot_raw = micro_count - 1 - tick_idx + (section_count - 1 - section_idx)
        active = (slot_raw >= 0) & (slot_raw < micro_count)
        slot_idx = jnp.clip(slot_raw, 0, micro_count - 1)
        grad_out = jnp.where(
            section_idx == section_count - 1,
            ends_in[0, max(micro_count - 1 - tick_idx, 0)],
            incoming_grad,
        ).astype(jnp.float32)
        cos_here = take_slot(rope_cos, slot_idx)
        sin_here = take_slot(rope_sin, slot_idx)
        mask_here = take_slot(allowed, slot_idx)
        key_all, value_all = (
            lax.all_gather(take_slot(keep_keys, slot_idx), "ctx", axis=1, tiled=True),
            lax.all_gather(take_slot(keep_values, slot_idx), "ctx", axis=1, tiled=True),
        )
        grad_queries, grad_keys, grad_values, grad_middle, grad_gain_b, tail_pieces = lax.cond(
            active,
            tail_backward,
            tail_back_skip,
            grad_out,
            take_slot(keep_middle, slot_idx),
            take_slot(keep_gate_up, slot_idx),
            take_slot(keep_attended, slot_idx),
            take_slot(keep_queries, slot_idx),
            take_slot(keep_lse, slot_idx),
            key_all,
            value_all,
            mask_here,
            full_bwd,
        )
        own_grad_keys, own_grad_values = (
            lax.psum_scatter(grad_keys, "ctx", scatter_dimension=1, tiled=True),
            lax.psum_scatter(grad_values, "ctx", scatter_dimension=1, tiled=True),
        )
        grad_residual, grad_gain_a, grad_bias, head_pieces = lax.cond(
            active,
            head_backward,
            head_skip,
            grad_queries,
            own_grad_keys,
            own_grad_values,
            grad_middle,
            take_slot(keep_residual, slot_idx),
            cos_here,
            sin_here,
            full_bwd,
        )
        if tick_idx + 1 < tick_count:
            incoming_grad = from_behind(grad_residual.astype(jnp.bfloat16), "section", -1)
        results = put_slot(results, grad_residual, slot_idx, active & (section_idx == 0))
        tick_gains = jnp.stack([grad_gain_a, grad_gain_b])
        pieces = head_pieces + tail_pieces
        gain_sums = gain_sums + tick_gains
        bias_sums = bias_sums + grad_bias
        keep_pieces = tuple(
            (
                put_slot(buffer, new_value, slot_idx, active)
                for buffer, new_value in zip(keep_pieces, pieces)
            )
        )
    total_gain, total_qkv, total_bias, total_out, total_in, total_down = weight_grads(
        gain_sums, bias_sums, keep_pieces
    )
    shard_sums = (
        lax.psum_scatter(total_gain, ("dp", "ctx"), scatter_dimension=1, tiled=True),
        lax.psum_scatter(total_qkv, ("dp", "ctx"), scatter_dimension=0, tiled=True),
        lax.psum_scatter(total_bias, ("dp", "ctx"), scatter_dimension=0, tiled=True),
        lax.psum_scatter(total_out, ("dp", "ctx"), scatter_dimension=0, tiled=True),
        lax.psum_scatter(total_in, ("dp", "ctx"), scatter_dimension=0, tiled=True),
        lax.psum_scatter(total_down, ("dp", "ctx"), scatter_dimension=0, tiled=True),
    )
    return (
        results[None],
        shard_sums[0][None],
        shard_sums[1][None],
        shard_sums[2][None],
        shard_sums[3][None],
        shard_sums[4][None],
        shard_sums[5][None],
    )


def solution(mesh):
    in_specs = (
        P("section", None, "dp", "ctx", None),
        P(None, "dp", "ctx"),
        P("section", None, ("dp", "ctx")),
        P("section", ("dp", "ctx"), None),
        P("section", ("dp", "ctx")),
        P("section", ("dp", "ctx"), None),
        P("section", ("dp", "ctx"), None),
        P("section", ("dp", "ctx"), None),
    )
    out_specs = (
        P("section", None, "dp", "ctx", None),
        P("section", None, ("dp", "ctx")),
        P("section", ("dp", "ctx"), None),
        P("section", ("dp", "ctx")),
        P("section", ("dp", "ctx"), None),
        P("section", ("dp", "ctx"), None),
        P("section", ("dp", "ctx"), None),
    )
    return jax.shard_map(
        per_device, mesh=mesh, in_specs=in_specs, out_specs=out_specs, check_vma=False
    )
```

profile of v0, /device:TPU:2, one launch (start us, length us, event | category | flops | bytes accessed | tf_op | source)
XLA Modules:
  0.0 2348.0 jit_solution(3810685832760256354)
XLA Ops:
  14.5 7.2 all_gather.62
  22.5 93.3 %all-gather = bf16[1,2,896]{1,0,2:T(2,128)(2,1)S(1)} all-gather(bf16[1,2,14]{1,0,2:T(2,128)(2,1)S(1)} %copy.320), channel_id=2, replica_groups=mesh['section'=2,'dp'=16,'ctx'=4] {'dp','ctx'}, dimensions={2}, use_global_device_ids=true | all-gather | bytes 3640 | tf_op jit(solution)/shard_map/all_gather | solution.py:297
  121.7 156.0 %all-reduce.1 = bf16[1152]{0:T(1024)(128)(2,1)S(1)} all-reduce(bf16[1152]{0:T(1024)(128)(2,1)S(1)} %dynamic-update-slice), channel_id=4, replica_groups=mesh['section'=2,'dp'=16,'ctx'=4] {'dp','ctx'}, use_global_device_ids=true, to_apply=%add.1 | all-reduce | flops 1152 | bytes 4608 | tf_op jit(solution)/shard_map/all_gather | solution.py:299
  288.0 16.7 conditional.12
  304.7 8.0 all_gather.66
  312.8 8.1 all_gather.67
  324.8 12.4 copy.437
  337.1 95.8 %all-gather.21.cloned.1.call-done = bf16[1,896,9728]{2,0,1:T(2,128)(2,1)} async-done(((bf16[1,14,9728]{2,0,1:T(2,128)(2,1)}), bf16[1,896,9728]{2,0,1:T(2,128)(2,1)}) %all-gather.21.cloned.1.call-update) | async-done | bytes 17432592 | tf_op jit(solution)/shard_map/all_gather | solution.py:301
  433.0 20.9 copy.436
  453.9 26.2 %conditional.13 = (f32[1,128,896]{2,1,0:T(8,128)}, f32[1,128,896]{2,1,0:T(8,128)}, f32[1,128,9728]{2,1,0:T(8,128)}, f32[1,2,7,128]{3,2,1,0:T(8,128)S(1)}, bf16[1,128,896]{2,1,0:T(8,128)(2,1)}) conditional(s32[]{:T(128)} %convert_element_type.660, () %tuple.134, (pred[1,128,512]{2,1,0:T(8,128)(4,1)S(1)}, bf16[1,512,128]{1,2,0:T(8,128)(2,1)}, ...), branch_computations={%region_5.6_spmd, %region_6.10_spmd} | conditional | flops 3800366336 | bytes 124193664 | solution.py:338
  470.8 7.5 fusion.20
  500.7 23.3 conditional.14
  524.1 7.4 all_gather.71
  531.5 7.3 all_gather.72
  539.6 26.8 %conditional.15 = (f32[1,128,896]{2,1,0:T(8,128)}, f32[1,128,896]{2,1,0:T(8,128)}, f32[1,128,9728]{2,1,0:T(8,128)}, f32[1,2,7,128]{3,2,1,0:T(8,128)S(1)}, bf16[1,128,896]{2,1,0:T(8,128)(2,1)}) conditional(s32[]{:T(128)} %convert_element_type.663, () %tuple.138, (pred[1,128,512]{2,1,0:T(8,128)(4,1)}, bf16[1,512,128]{1,2,0:T(8,128)(2,1)}, ...), branch_computations={%region_13.14_spmd, %region_14.18_spmd} | conditional | flops 3800366336 | bytes 124980128 | solution.py:338
  557.1 7.5 fusion.49
  595.3 7.4 all_gather.73
  612.4 7.4 all-gather.6
  622.7 7.4 all-gather.7
  643.8 9.1 conditional.18
  653.0 7.6 all-gather.8
  660.6 7.6 all-gather.9
  668.2 8.1 all-gather.10
  693.1 7.4 all-gather.11
  708.2 49.4 %reduce-scatter.16.cloned.1.call-done = f32[1,128,128]{1,2,0:T(8,128)} async-done(((f32[1,512,128]{1,2,0:T(8,128)}), f32[1,128,128]{1,2,0:T(8,128)}) %reduce-scatter.16.cloned.1.call-update) | async-done | bytes 65552 | tf_op jit(solution)/shard_map/reduce_scatter | solution.py:414
  757.6 44.8 %reduce-scatter.18.cloned.1.call-done = f32[1,128,128]{1,2,0:T(8,128)} async-done(((f32[1,512,128]{1,2,0:T(8,128)}), f32[1,128,128]{1,2,0:T(8,128)}) %reduce-scatter.18.cloned.1.call-update) | async-done | bytes 65552 | tf_op jit(solution)/shard_map/reduce_scatter | solution.py:415
  820.4 48.1 %conditional.20 = (f32[1,128,896]{1,2,0:T(8,128)}, f32[1,512,128]{1,2,0:T(8,128)}, f32[1,512,128]{1,2,0:T(8,128)}, f32[1,128,896]{2,1,0:T(8,128)}, bf16[1,128,89...) conditional(s32[]{:T(128)} %convert_element_type.663, ...), branch_computations={%region_40.41_spmd, %region_41.46_spmd} | conditional | flops 4172381184 | bytes 155961472 | solution.py:398
  837.6 13.0 fusion.158
  902.1 26.5 %reduce-scatter.22.cloned.1.call-done = f32[1,128,128]{1,2,0:T(8,128)} async-done(((f32[1,512,128]{1,2,0:T(8,128)}), f32[1,128,128]{1,2,0:T(8,128)}) %reduce-scatter.22.cloned.1.call-update) | async-done | bytes 65552 | tf_op jit(solution)/shard_map/reduce_scatter | solution.py:415
  928.6 7.5 conditional.21
  953.1 45.6 %conditional.22 = (f32[1,128,896]{1,2,0:T(8,128)}, f32[1,512,128]{1,2,0:T(8,128)}, f32[1,512,128]{1,2,0:T(8,128)}, f32[1,128,896]{2,1,0:T(8,128)}, bf16[1,128,89...) conditional(s32[]{:T(128)} %convert_element_type.660, ...), branch_computations={%region_54.55_spmd, %region_55.60_spmd} | conditional | flops 4172381184 | bytes 155043936 | solution.py:398
  970.4 13.0 fusion.205
  1005.6 9.3 convolution_bitcast_fusion.10
  1014.9 215.9 %fusion.3 = f32[80,896]{1,0:T(8,128)} fusion(f32[4864,896]{1,0:T(8,128)} %convolution_bitcast_fusion.10), kind=kCustom, calls=%all-reduce-scatter.3 | all-reduce-scatter fusion | flops 4587521 | bytes 17719808
  1237.4 7.2 collective-permute-start.29
  1255.5 18.9 convolution_bitcast_fusion.9
  1275.2 8.1 conditional.23
  1294.5 510.0 %fusion.269 = (f32[16,1152]{1,0:T(8,128)S(1)}, f32[16,896]{1,0:T(8,128)S(1)}, f32[16,9728]{1,0:T(8,128)S(1)}) fusion(f32[896,1152]{1,0:T(8,128)} %convolution_bitcast_fusion.11, f32[896,896]{1,0:T(8,128)} %convolution_bitcast_fusion.12, f32[896,9728]{1,0:T(8,128)} %convolution_bitcast_fusion.9), kind=kCustom, calls=%all-reduce-scatter.4 | all-reduce-scatter fusion | flops 12058625 | bytes 42959360
  1804.6 9.6 collective-permute-start.18
  1814.2 8.0 collective-permute-start.17
  1844.9 8.3 collective-permute-start.26
  1876.8 15.4 collective-permute-start.9
  1895.7 8.2 collective-permute-start.7
  1906.6 312.2 %all-reduce.12 = (f32[2,896]{1,0:T(2,128)S(1)}, f32[1152]{0:T(1024)S(1)}) all-reduce(f32[2,896]{1,0:T(2,128)S(1)} %fusion.264, f32[1152]{0:T(1024)S(1)} %add_add_fusion.6), channel_id=20, replica_groups=mesh['section'=2,'dp'=16,'ctx'=4] {'dp','ctx'}, use_global_device_ids=true, to_apply=%region_68.69.clone | all-reduce | flops 2944 | bytes 23552
  2223.5 7.5 collective-permute-done.5
  2253.2 11.7 collective-permute-done.23
  2267.7 24.5 %collective-permute-done.21 = f32[16,9728]{1,0:T(8,128)} collective-permute-done((f32[16,9728]{1,0:T(8,128)S(1)}, f32[16,9728]{1,0:T(8,128)}, u32[]{:S(2)}, u32[]{:S(2)}) %collective-permute-start.21) | collective-permute-done | bytes 622624
  2292.2 45.9 %concatenate.263 = f32[142,9728]{1,0:T(8,128)} concatenate(f32[14,9728]{1,0:T(8,128)} %collective-permute-done.27, f32[16,9728]{1,0:T(8,128)} %collective-permute-done.26, f32[16,9728]{1,0:T(8,128)} %collective-permute-done.25, f32[16,9728]{1,0:T(8,128)S(1)} %collective-permute-done.24, f32[16,9728]{1,0:T(8,128)} %collective-permute-done.23, ...), dimensions={0} | concatenate | bytes 11051008
  (704 shorter events, 490.1 us)
Async XLA Ops:
  7.2 114.2 %copy-start.144 = (bf16[1,18]{1,0:T(2,128)(2,1)S(1)}, bf16[1,18]{1,0:T(2,128)(2,1)}, u32[]{:S(2)}) copy-start(bf16[1,18]{1,0:T(2,128)(2,1)} %param.36) | copy-start | bytes 112
  7.2 273.0 %copy-start.24 = (bf16[1,2,1,128,896]{4,3,2,1,0:T(8,128)(2,1)S(1)}, bf16[1,2,1,128,896]{4,3,2,1,0:T(8,128)(2,1)}, u32[]{:S(2)}) copy-start(bf16[1,2,1,128,896]{4,3,2,1,0:T(8,128)(2,1)} %param.32) | copy-start | bytes 1376260
  7.2 274.7 %all-gather.19.cloned.1.call-start = ((), (), s32[]{:S(2)}) async-start(), calls=%async_computation.13 | async-start | bytes 3261440 | tf_op jit(solution)/shard_map/all_gather | solution.py:300
  8.7 275.4 %all-gather.17.cloned.1.call-start = ((), (), s32[]{:S(2)}) async-start(), calls=%async_computation.12 | async-start | bytes 4193280 | tf_op jit(solution)/shard_map/all_gather | solution.py:298
  10.2 314.6 %all-gather.23.cloned.1.call-start = ((), (), s32[]{:S(2)}) async-start(), calls=%async_computation.15 | async-start | bytes 17704960 | tf_op jit(solution)/shard_map/all_gather | solution.py:302
  12.1 420.8 %all-gather.21.cloned.1.call-start = ((), (), s32[]{:S(2)}) async-start(), calls=%async_computation.14 | async-start | bytes 35409920 | tf_op jit(solution)/shard_map/all_gather | solution.py:301
  14.4 743.2 %reduce-scatter.16.cloned.1.call-start = ((), (), s32[]{:S(2)}) async-start(), calls=%async_computation.6 | async-start | bytes 327680 | tf_op jit(solution)/shard_map/reduce_scatter | solution.py:414
  280.1 173.7 %copy-start.50 = (pred[1,128,512]{2,1,0:T(8,128)(4,1)}, pred[1,128,512]{2,1,0:T(8,128)(4,1)S(1)}, u32[]{:S(2)}) copy-start(pred[1,128,512]{2,1,0:T(8,128)(4,1)S(1)} %get-tuple-element.1545) | copy-start | bytes 196612
  481.1 19.5 collective-permute-start
  567.5 26.9 %collective-permute-start.1 = (bf16[1,128,896]{2,1,0:T(8,128)(2,1)S(1)}, bf16[1,128,896]{2,1,0:T(8,128)(2,1)S(1)}, u32[]{:S(2)}, u32[]{:S(2)}) collective-permute-start(bf16[1,128,896]{2,1,0:T(8,128)(2,1)S(1)} %convert_element_type.667), channel_id=1, source_target_pairs={{0,64},{1,65},{2,66},{3,67},{4,68},{5,69},{6,70},{7,71},{8,72},{9,... | collective-permute-start | bytes 688136 | tf_op jit(solution)/shard_map/ppermute | solution.py:20
  652.9 149.5 %reduce-scatter.18.cloned.1.call-start = ((), (), s32[]{:S(2)}) async-start(), calls=%async_computation.7 | async-start | bytes 327680 | tf_op jit(solution)/shard_map/reduce_scatter | solution.py:415
  691.5 111.0 %copy-start.98 = (f32[1,128,1,64]{1,3,2,0:T(8,128)S(1)}, f32[1,128,1,64]{1,3,2,0:T(8,128)}, u32[]{:S(2)}) copy-start(f32[1,128,1,64]{1,3,2,0:T(8,128)} %get-tuple-element.1555) | copy-start | bytes 98308
  691.5 210.6 %reduce-scatter.20.cloned.1.call-start = ((), (), s32[]{:S(2)}) async-start(), calls=%async_computation.8 | async-start | bytes 327680 | tf_op jit(solution)/shard_map/reduce_scatter | solution.py:414
  803.4 15.1 collective-permute-start.2
  868.5 60.1 %reduce-scatter.22.cloned.1.call-start = ((), (), s32[]{:S(2)}) async-start(), calls=%async_computation.9 | async-start | bytes 327680 | tf_op jit(solution)/shard_map/reduce_scatter | solution.py:415
  878.8 395.5 %reduce-scatter.24.cloned.1.call-start = ((), (), s32[]{:S(2)}) async-start(), calls=%async_computation.10 | async-start | bytes 327680 | tf_op jit(solution)/shard_map/reduce_scatter | solution.py:414
  937.6 13.6 collective-permute-start.3
  998.7 276.5 %reduce-scatter.26.cloned.1.call-start = ((), (), s32[]{:S(2)}) async-start(), calls=%async_computation.11 | async-start | bytes 327680 | tf_op jit(solution)/shard_map/reduce_scatter | solution.py:415
  1232.2 590.0 %collective-permute-start.30 = (f32[80,896]{1,0:T(8,128)}, f32[80,896]{1,0:T(8,128)}, u32[]{:S(2)}, u32[]{:S(2)}) collective-permute-start(f32[80,896]{1,0:T(8,128)} %fusion.3), channel_id=1, source_target_pairs={{0,3},{1,4},{2,5},{3,6},{4,7},{5,8},{6,9},{7,10},{8,11},{9,12},{10... | collective-permute-start | bytes 860168
  1237.4 589.4 %collective-permute-start.29 = (f32[80,896]{1,0:T(8,128)}, f32[80,896]{1,0:T(8,128)}, u32[]{:S(2)}, u32[]{:S(2)}) collective-permute-start(f32[80,896]{1,0:T(8,128)} %fusion.3), channel_id=1, source_target_pairs={{0,2},{1,3},{2,4},{3,5},{4,6},{5,7},{6,8},{7,9},{8,10},{9,11},{10,... | collective-permute-start | bytes 860168
  1244.7 585.3 %collective-permute-start.28 = (f32[80,896]{1,0:T(8,128)}, f32[80,896]{1,0:T(8,128)}, u32[]{:S(2)}, u32[]{:S(2)}) collective-permute-start(f32[80,896]{1,0:T(8,128)} %fusion.3), channel_id=1, source_target_pairs={{0,1},{1,2},{2,3},{3,4},{4,5},{5,6},{6,7},{7,8},{8,9},{9,10},{10,1... | collective-permute-start | bytes 860168
  1246.8 567.4 %collective-permute-start.31 = (f32[12,896]{1,0:T(8,128)}, f32[12,896]{1,0:T(8,128)}, u32[]{:S(2)}, u32[]{:S(2)}) collective-permute-start(f32[12,896]{1,0:T(8,128)} %slice.286), channel_id=1, source_target_pairs={{0,4},{1,5},{2,6},{3,7},{4,8},{5,9},{6,10},{7,11},{8,12},{9,13},{1... | collective-permute-start | bytes 129032
  1294.5 539.1 %copy-start.16 = (f32[2,1,128,896]{3,2,0,1:T(8,128)S(1)}, f32[2,1,128,896]{3,2,0,1:T(8,128)}, u32[]{:S(2)}) copy-start(f32[2,1,128,896]{3,2,0,1:T(8,128)} %bitcast_dynamic-update-slice_fusion.13) | copy-start | bytes 2752516
  1294.5 565.1 %copy-start.46 = (f32[1,128,896]{2,1,0:T(8,128)S(1)}, f32[1,128,896]{2,1,0:T(8,128)}, u32[]{:S(2)}) copy-start(f32[1,128,896]{2,1,0:T(8,128)} %copy-done.45) | copy-start | bytes 1376260
  1804.6 35.7 %collective-permute-start.18 = (f32[16,896]{1,0:T(8,128)S(1)}, f32[16,896]{1,0:T(8,128)S(1)}, u32[]{:S(2)}, u32[]{:S(2)}) collective-permute-start(f32[16,896]{1,0:T(8,128)S(1)} %get-tuple-element.1451), channel_id=1, source_target_pairs={{0,7},{1,8},{2,9},{3,10},{4,11},{5,12},{6,13},{7,14},{8,15},{9,16}... | collective-permute-start | bytes 172040
  1814.2 28.7 %collective-permute-start.17 = (f32[16,896]{1,0:T(8,128)S(1)}, f32[16,896]{1,0:T(8,128)S(1)}, u32[]{:S(2)}, u32[]{:S(2)}) collective-permute-start(f32[16,896]{1,0:T(8,128)S(1)} %get-tuple-element.1451), channel_id=1, source_target_pairs={{0,6},{1,7},{2,8},{3,9},{4,10},{5,11},{6,12},{7,13},{8,14},{9,15},... | collective-permute-start | bytes 172040
  1822.3 22.6 collective-permute-start.16
  1826.9 26.4 %collective-permute-start.15 = (f32[16,896]{1,0:T(8,128)S(1)}, f32[16,896]{1,0:T(8,128)S(1)}, u32[]{:S(2)}, u32[]{:S(2)}) collective-permute-start(f32[16,896]{1,0:T(8,128)S(1)} %get-tuple-element.1451), channel_id=1, source_target_pairs={{0,4},{1,5},{2,6},{3,7},{4,8},{5,9},{6,10},{7,11},{8,12},{9,13},{1... | collective-permute-start | bytes 172040
  1830.0 5.5 collective-permute-start.19
  1835.4 30.4 %collective-permute-start.14 = (f32[16,896]{1,0:T(8,128)S(1)}, f32[16,896]{1,0:T(8,128)}, u32[]{:S(2)}, u32[]{:S(2)}) collective-permute-start(f32[16,896]{1,0:T(8,128)S(1)} %get-tuple-element.1451), channel_id=1, source_target_pairs={{0,3},{1,4},{2,5},{3,6},{4,7},{5,8},{6,9},{7,10},{8,11},{9,12},{10... | collective-permute-start | bytes 172040
  1840.3 26.8 %collective-permute-start.13 = (f32[16,896]{1,0:T(8,128)S(1)}, f32[16,896]{1,0:T(8,128)}, u32[]{:S(2)}, u32[]{:S(2)}) collective-permute-start(f32[16,896]{1,0:T(8,128)S(1)} %get-tuple-element.1451), channel_id=1, source_target_pairs={{0,2},{1,3},{2,4},{3,5},{4,6},{5,7},{6,8},{7,9},{8,10},{9,11},{10,... | collective-permute-start | bytes 172040
  1843.0 29.2 %collective-permute-start.12 = (f32[16,896]{1,0:T(8,128)S(1)}, f32[16,896]{1,0:T(8,128)}, u32[]{:S(2)}, u32[]{:S(2)}) collective-permute-start(f32[16,896]{1,0:T(8,128)S(1)} %get-tuple-element.1451), channel_id=1, source_target_pairs={{0,1},{1,2},{2,3},{3,4},{4,5},{5,6},{6,7},{7,8},{8,9},{9,10},{10,1... | collective-permute-start | bytes 172040
  1844.9 391.3 %collective-permute-start.26 = (f32[16,9728]{1,0:T(8,128)S(1)}, f32[16,9728]{1,0:T(8,128)}, u32[]{:S(2)}, u32[]{:S(2)}) collective-permute-start(f32[16,9728]{1,0:T(8,128)S(1)} %get-tuple-element.1452), channel_id=1, source_target_pairs={{0,7},{1,8},{2,9},{3,10},{4,11},{5,12},{6,13},{7,14},{8,15},{9,16}... | collective-permute-start | bytes 1867784
  1853.2 384.9 %collective-permute-start.25 = (f32[16,9728]{1,0:T(8,128)S(1)}, f32[16,9728]{1,0:T(8,128)}, u32[]{:S(2)}, u32[]{:S(2)}) collective-permute-start(f32[16,9728]{1,0:T(8,128)S(1)} %get-tuple-element.1452), channel_id=1, source_target_pairs={{0,6},{1,7},{2,8},{3,9},{4,10},{5,11},{6,12},{7,13},{8,14},{9,15},... | collective-permute-start | bytes 1867784
  1865.8 27.4 %collective-permute-start.10 = (f32[16,1152]{1,0:T(8,128)S(1)}, f32[16,1152]{1,0:T(8,128)S(1)}, u32[]{:S(2)}, u32[]{:S(2)}) collective-permute-start(f32[16,1152]{1,0:T(8,128)S(1)} %get-tuple-element.1450), channel_id=1, source_target_pairs={{0,7},{1,8},{2,9},{3,10},{4,11},{5,12},{6,13},{7,14},{8,15},{9,16}... | collective-permute-start | bytes 221192
  1867.1 9.7 collective-permute-start.11
  1872.2 362.1 %collective-permute-start.27 = (f32[14,9728]{1,0:T(8,128)S(1)}, f32[14,9728]{1,0:T(8,128)}, u32[]{:S(2)}, u32[]{:S(2)}) collective-permute-start(f32[14,9728]{1,0:T(8,128)S(1)} %slice.285), channel_id=1, source_target_pairs={{0,8},{1,9},{2,10},{3,11},{4,12},{5,13},{6,14},{7,15},{8,16},{9,17... | collective-permute-start | bytes 1634312
  1876.8 19.0 collective-permute-start.9
  1893.2 10.7 collective-permute-start.8
  1895.7 323.0 %collective-permute-start.7 = (f32[16,1152]{1,0:T(8,128)S(1)}, f32[16,1152]{1,0:T(8,128)S(1)}, u32[]{:S(2)}, u32[]{:S(2)}) collective-permute-start(f32[16,1152]{1,0:T(8,128)S(1)} %get-tuple-element.1450), channel_id=1, source_target_pairs={{0,4},{1,5},{2,6},{3,7},{4,8},{5,9},{6,10},{7,11},{8,12},{9,13},{1... | collective-permute-start | bytes 221192
  1903.9 316.8 %collective-permute-start.6 = (f32[16,1152]{1,0:T(8,128)S(1)}, f32[16,1152]{1,0:T(8,128)S(1)}, u32[]{:S(2)}, u32[]{:S(2)}) collective-permute-start(f32[16,1152]{1,0:T(8,128)S(1)} %get-tuple-element.1450), channel_id=1, source_target_pairs={{0,3},{1,4},{2,5},{3,6},{4,7},{5,8},{6,9},{7,10},{8,11},{9,12},{10... | collective-permute-start | bytes 221192
  2218.8 12.2 collective-permute-start.5
  2220.7 11.6 collective-permute-start.4
  2231.0 22.3 collective-permute-start.24
  2232.3 32.6 %collective-permute-start.23 = (f32[16,9728]{1,0:T(8,128)S(1)}, f32[16,9728]{1,0:T(8,128)}, u32[]{:S(2)}, u32[]{:S(2)}) collective-permute-start(f32[16,9728]{1,0:T(8,128)S(1)} %get-tuple-element.1452), channel_id=1, source_target_pairs={{0,4},{1,5},{2,6},{3,7},{4,8},{5,9},{6,10},{7,11},{8,12},{9,13},{1... | collective-permute-start | bytes 1867784
  2234.3 33.4 %collective-permute-start.22 = (f32[16,9728]{1,0:T(8,128)S(1)}, f32[16,9728]{1,0:T(8,128)S(1)}, u32[]{:S(2)}, u32[]{:S(2)}) collective-permute-start(f32[16,9728]{1,0:T(8,128)S(1)} %get-tuple-element.1452), channel_id=1, source_target_pairs={{0,3},{1,4},{2,5},{3,6},{4,7},{5,8},{6,9},{7,10},{8,11},{9,12},{10... | collective-permute-start | bytes 1867784
  2236.2 56.0 %collective-permute-start.21 = (f32[16,9728]{1,0:T(8,128)S(1)}, f32[16,9728]{1,0:T(8,128)}, u32[]{:S(2)}, u32[]{:S(2)}) collective-permute-start(f32[16,9728]{1,0:T(8,128)S(1)} %get-tuple-element.1452), channel_id=1, source_target_pairs={{0,2},{1,3},{2,4},{3,5},{4,6},{5,7},{6,8},{7,9},{8,10},{9,11},{10,... | collective-permute-start | bytes 1867784
  2238.1 54.1 %collective-permute-start.20 = (f32[16,9728]{1,0:T(8,128)S(1)}, f32[16,9728]{1,0:T(8,128)}, u32[]{:S(2)}, u32[]{:S(2)}) collective-permute-start(f32[16,9728]{1,0:T(8,128)S(1)} %get-tuple-element.1452), channel_id=1, source_target_pairs={{0,1},{1,2},{2,3},{3,4},{4,5},{5,6},{6,7},{7,8},{8,9},{9,10},{10,1... | collective-permute-start | bytes 1867784
  (122 other events, 961.0 us)
Sparse Core Ops, SparseCore 0:
  11.7 72.1 all-gather.18
  87.6 70.1 all-gather.16
  161.5 106.9 all-gather.22
  271.9 161.0 all-gather.20
  653.1 104.5 reduce-scatter.15
  760.2 42.1 reduce-scatter.17
  868.7 30.8 reduce-scatter.19
  902.3 26.2 reduce-scatter.21
  998.8 29.4 reduce-scatter.23
  1248.9 26.2 reduce-scatter.25
where the time goes:
time: 2360 us; the launch traced here: 2350 us
  blocking collectives  1390 us (59%)
  local copies, waits for them, and re-layouts  290 us (12%)
  waiting for transfers between devices  271 us (11%)
  matrix products  136 us (6%)
  starting transfers between devices  125 us (5%)
  other arithmetic  120 us (5%)
    unnamed x3, blocking collectives  1040 us
    all_gather x1, blocking collectives, per_device(): lax.all_gather(qkv_bias[0], ('dp', 'ctx'), axis=0, tiled=True)  156 us
    unnamed x224, local copies, waits for them, and re-layouts  140 us
    unnamed x28, starting transfers between devices  119 us
    all_gather x1, waiting for transfers between devices, per_device(): lax.all_gather(in_weight[0], ('dp', 'ctx'), axis=0, tiled=True)  95.8 us
    all_gather x1, blocking collectives, per_device(): lax.all_gather(norm_gains[0], ('dp', 'ctx'), axis=1, tiled=True)  93.3 us
    reduce_scatter x3, waiting for transfers between devices, per_device(): lax.psum_scatter(grad_values, 'ctx', scatter_dimension=1, tiled=True)  72.2 us
    dynamic_update_slice x46, other arithmetic, put_slot(): lax.dynamic_update_index_in_dim(buffer, jnp.where(active, new_value, take...  60.5 us
  transfers between devices with their start and end apart: 42, of which 13 were waited for; matrix products, arithmetic and copies ran while one was open for 41% of the time, Pallas kernels for 0%

commit v1 on v0

v1 whole, which is shorter than its diff:
```python
import jax
import jax.numpy as jnp
from jax import lax
from jax.experimental import pallas as pl
from jax.experimental.pallas import tpu as pltpu
from jax.sharding import PartitionSpec as P

MESH = pl.DeviceIdType.MESH
HEADS = 14
HEAD = 64
D = 896
DP = 1024
QKV = 1152
FF = 4864
FP = 5120
ROWS = 128
WIDE = 2 * FP + QKV + D
GATE = QKV + D
TILE = 512
EPS = 1e-06
BF = jnp.bfloat16
F32 = jnp.float32
ANY = pl.BlockSpec(memory_space=pl.ANY)
VM = pl.BlockSpec(memory_space=pltpu.VMEM)


def place():
    dp, ctx = lax.axis_index("dp"), lax.axis_index("ctx")
    core, zh = lax.rem(ctx, 2), ctx // 2
    y, x = dp // 4, lax.rem(dp, 4)
    one = core * y + (1 - core) * x
    two = core * x + (1 - core) * y
    return core, zh, one, two

def dp_at(core, one, two):
    return two * (4 - 3 * core) + one * (1 + 3 * core)

def ids(core, zh, one, two):
    return {"dp": dp_at(core, one, two), "ctx": 2 * zh + core}

def gather_kernel(wd, wn, gd, gn, send, recv, loc):
    core, zh, one, two = place()
    ring = lambda p: lax.rem(p + 8, 4)
    sib = {"dp": dp_at(core, one, two), "ctx": 2 * zh + 1 - core}
    zpart = ids(core, 1 - zh, one, two)
    barrier = pltpu.get_barrier_semaphore()
    for other in (sib, zpart, ids(core, zh, ring(one + 1), two), ids(core, zh, ring(one - 1), two),
                  ids(core, zh, one, ring(two + 1)), ids(core, zh, one, ring(two - 1))):
        pl.semaphore_signal(barrier, inc=1, device_id=other, device_id_type=MESH)
    pl.semaphore_wait(barrier, 6)
    hs = (zh, 1 - zh)
    started = []

    def shard(q1, q2, h):
        return 4 * dp_at(core, q1, q2) + 2 * h + core

    def copies(src, s, msg, dev):
        d0, n0 = src
        out = []
        for i, (a, g) in enumerate(((d0, gd), (n0, gn))):
            out.append(pltpu.make_async_remote_copy(src_ref=a, dst_ref=g.at[s], send_sem=send.at[2 * msg + i],
                       recv_sem=recv.at[2 * msg + i], device_id=dev, device_id_type=MESH))
        return out

    def go(src, s, msg, dev):
        for c in copies(src, s, msg, dev):
            c.start()
            started.append(c)

    def held(s):
        return gd.at[s], gn.at[s]

    def arrive(s, msg):
        for c in copies(held(s), s, msg, sib):
            c.wait_recv()

    A, B, D = 0, 1, 2
    m1 = lambda k, kind: 1 + 3 * k + kind
    m2 = lambda j, k, kind: 7 + (2 * j + k) * 3 + kind
    m3 = lambda j, k, t: 31 + (2 * j + k) * 4 + t

    own = shard(one, two, zh)
    lc = [pltpu.make_async_copy(wd, gd.at[own], loc.at[0]), pltpu.make_async_copy(wn, gn.at[own], loc.at[1])]
    for c in lc:
        c.start()

    dirs = [1 - 2 * h for h in hs]
    def pos(k, j, p):
        return ring(p + (0, -dirs[k], dirs[k], 2)[j])

    def spread(k, j, src):
        q1 = pos(k, j, one)
        s = shard(q1, two, hs[k])
        go(src, s, m2(j, k, A), ids(core, zh, one, ring(two + dirs[k])))
        go(src, s, m2(j, k, B), ids(core, zh, one, ring(two - dirs[k])))
        go(src, s, m3(j, k, 0), sib)

    def first(k, src):
        s = shard(one, two, hs[k])
        go(src, s, m1(k, A), ids(core, zh, ring(one + dirs[k]), two))
        go(src, s, m1(k, B), ids(core, zh, ring(one - dirs[k]), two))
        spread(k, 0, src)

    src = (wd, wn)
    go(src, own, 0, zpart)
    first(0, src)
    s = shard(one, two, hs[1])
    arrive(s, 0)
    first(1, held(s))
    for k in (0, 1):
        s = shard(pos(k, 1, one), two, hs[k])
        arrive(s, m1(k, A))
        go(held(s), s, m1(k, D), ids(core, zh, ring(one + dirs[k]), two))
        spread(k, 1, held(s))
        s = shard(pos(k, 2, one), two, hs[k])
        arrive(s, m1(k, B))
        spread(k, 2, held(s))
    for k in (0, 1):
        s = shard(pos(k, 3, one), two, hs[k])
        arrive(s, m1(k, D))
        spread(k, 3, held(s))
    for j in range(4):
        for k in (0, 1):
            q1 = pos(k, j, one)
            s = shard(q1, pos(k, 1, two), hs[k])
            arrive(s, m2(j, k, A))
            go(held(s), s, m2(j, k, D), ids(core, zh, one, ring(two + dirs[k])))
            go(held(s), s, m3(j, k, 1), sib)
            s = shard(q1, pos(k, 2, two), hs[k])
            arrive(s, m2(j, k, B))
            go(held(s), s, m3(j, k, 2), sib)
    for j in range(4):
        for k in (0, 1):
            s = shard(pos(k, j, one), pos(k, 3, two), hs[k])
            arrive(s, m2(j, k, D))
            go(held(s), s, m3(j, k, 3), sib)
    oc, o1, o2 = 1 - core, two, one
    for j in range(4):
        for k in (0, 1):
            for t in range(4):
                s = 4 * dp_at(oc, pos(k, j, o1), pos(k, t, o2)) + 2 * hs[k] + oc
                arrive(s, m3(j, k, t))
    for c in started:
        c.wait_send()
    for c in lc:
        c.wait()

def gather(wd, wn):
    return pl.pallas_call(
        gather_kernel,
        out_shape=(jax.ShapeDtypeStruct((64,) + wd.shape, wd.dtype), jax.ShapeDtypeStruct((64,) + wn.shape, wn.dtype)),
        in_specs=[pl.BlockSpec(memory_space=pl.ANY)] * 2,
        out_specs=(pl.BlockSpec(memory_space=pl.ANY),) * 2,
        scratch_shapes=[pltpu.SemaphoreType.DMA((126,)), pltpu.SemaphoreType.DMA((126,)), pltpu.SemaphoreType.DMA((2,))],
        compiler_params=pltpu.CompilerParams(collective_id=0, has_side_effects=True),
        name="gather",
    )(wd, wn)


def scatter_kernel(pd, pn, od, on, sd, sn, rd, rn, td, tn, fd, fn, send, recv, loc, oloc):
    core, zh, one, two = place()
    ring = lambda p: lax.rem(p + 8, 4)
    oc = 1 - core
    sib = {"dp": dp_at(core, one, two), "ctx": 2 * zh + oc}
    zpart = ids(core, 1 - zh, one, two)
    barrier = pltpu.get_barrier_semaphore()
    for other in (sib, zpart, ids(core, zh, ring(one + 1), two), ids(core, zh, ring(one - 1), two),
                  ids(core, zh, one, ring(two + 1)), ids(core, zh, one, ring(two - 1))):
        pl.semaphore_signal(barrier, inc=1, device_id=other, device_id_type=MESH)
    pl.semaphore_wait(barrier, 6)
    hs = (zh, 1 - zh)
    dirs = [1 - 2 * h for h in hs]
    started = []
    A, B, D = 0, 1, 2

    def copies(src, dst, msg, dev):
        return [pltpu.make_async_remote_copy(src_ref=a, dst_ref=g, send_sem=send.at[2 * msg + i],
                recv_sem=recv.at[2 * msg + i], device_id=dev, device_id_type=MESH)
                for i, (a, g) in enumerate(zip(src, dst))]

    def go(src, dst, msg, dev):
        for c in copies(src, dst, msg, dev):
            c.start()
            started.append(c)

    def arrive(dst, msg):
        for c in copies(dst, dst, msg, sib):
            c.wait_recv()

    def pos(k, j, p):
        return ring(p + (0, -dirs[k], dirs[k], 2)[j])

    def add(dst, src):
        def body(i, _):
            c = pl.ds(pl.multiple_of(i * 1024, 1024), 1024)
            dst[0][:, c] = dst[0][:, c] + src[0][:, c]
            return 0
        lax.fori_loop(0, 12, body, 0)
        dst[1][...] = dst[1][...] + src[1][...]

    order = [(j, k) for j in (3, 2, 1, 0) for k in (1, 0)]
    ts = (3, 2, 1, 0)
    sslot = lambda j, k, t: (2 * j + k) * 4 + t
    for j, k in order:
        for t in ts:
            s = 4 * dp_at(oc, pos(k, j, two), pos(k, t, one)) + 2 * hs[k] + oc
            n = sslot(j, k, t)
            go((pd.at[s], pn.at[s]), (sd.at[n], sn.at[n]), n, sib)
    m2 = lambda j, k, kind: 32 + (2 * j + k) * 3 + kind
    m1 = lambda k, kind: 56 + 3 * k + kind
    rslot = lambda m: (rd.at[m - 32], rn.at[m - 32])
    mz = 62

    flat = [(j, k, t) for j, k in order for t in ts]
    def fetch(n):
        j, k, t = flat[n]
        s = 4 * dp_at(core, pos(k, j, one), pos(k, t, two)) + 2 * hs[k] + core
        b = n % 4
        return [pltpu.make_async_copy(pd.at[s], td.at[b], loc.at[b, 0]), pltpu.make_async_copy(pn.at[s], tn.at[b], loc.at[b, 1])]
    for n in range(4):
        for c in fetch(n):
            c.start()

    def piece(n):
        j, k, t = flat[n]
        m = sslot(j, k, t)
        here = (sd.at[m], sn.at[m])
        for c in fetch(n):
            c.wait()
        arrive(here, m)
        add(here, (td.at[n % 4], tn.at[n % 4]))
        if n + 4 < len(flat):
            for c in fetch(n + 4):
                c.start()
        return here

    sums = {}
    def two_start(g):
        j, k = order[g]
        for i, t in enumerate(ts):
            here = piece(4 * g + i)
            sums[j, k, t] = here
            if t == 3:
                m = m2(j, k, D)
                go(here, rslot(m), m, ids(core, zh, one, ring(two - dirs[k])))
            if t == 2:
                m = m2(j, k, B)
                go(here, rslot(m), m, ids(core, zh, one, ring(two + dirs[k])))

    def two_mid(g):
        j, k = order[g]
        here = sums[j, k, 1]
        got = rslot(m2(j, k, D))
        arrive(got, m2(j, k, D))
        add(here, got)
        m = m2(j, k, A)
        go(here, rslot(m), m, ids(core, zh, one, ring(two - dirs[k])))

    def two_end(g):
        j, k = order[g]
        here = sums[j, k, 0]
        for kind in (B, A):
            got = rslot(m2(j, k, kind))
            arrive(got, m2(j, k, kind))
            add(here, got)
        if j == 3:
            m = m1(k, D)
            go(here, rslot(m), m, ids(core, zh, ring(one - dirs[k]), two))
        if j == 2:
            m = m1(k, B)
            go(here, rslot(m), m, ids(core, zh, ring(one + dirs[k]), two))
        if j == 1:
            got = rslot(m1(k, D))
            arrive(got, m1(k, D))
            add(here, got)
            m = m1(k, A)
            go(here, rslot(m), m, ids(core, zh, ring(one - dirs[k]), two))
        if j == 0:
            for kind in (B, A):
                got = rslot(m1(k, kind))
                arrive(got, m1(k, kind))
                add(here, got)
            if k == 1:
                go(here, rslot(mz), mz, zpart)
            else:
                got = rslot(mz)
                arrive(got, mz)
                def body(i, _):
                    c = pl.ds(pl.multiple_of(i * 1024, 1024), 1024)
                    fd[:, c] = here[0][:, c].astype(jnp.float32) + got[0][:, c].astype(jnp.float32)
                    return 0
                lax.fori_loop(0, 12, body, 0)
                fn[...] = here[1][...].astype(jnp.float32) + got[1][...].astype(jnp.float32)
                last = [pltpu.make_async_copy(fd, od, oloc.at[0]), pltpu.make_async_copy(fn, on, oloc.at[1])]
                for c in last:
                    c.start()
                for c in last:
                    c.wait()

    for step in range(len(order) + 2):
        if step < len(order):
            two_start(step)
        if 0 <= step - 1 < len(order):
            two_mid(step - 1)
        if 0 <= step - 2:
            two_end(step - 2)
    for c in started:
        c.wait_send()

def scatter(pd, pn):
    bf = jnp.bfloat16
    return pl.pallas_call(
        scatter_kernel,
        out_shape=(jax.ShapeDtypeStruct(pd.shape[1:], jnp.float32), jax.ShapeDtypeStruct(pn.shape[1:], jnp.float32)),
        in_specs=[pl.BlockSpec(memory_space=pl.ANY)] * 2,
        out_specs=(pl.BlockSpec(memory_space=pl.ANY),) * 2,
        scratch_shapes=[
            pltpu.VMEM((32, 16, 12288), bf), pltpu.VMEM((32, 80, 896), bf),
            pltpu.VMEM((31, 16, 12288), bf), pltpu.VMEM((31, 80, 896), bf),
            pltpu.VMEM((4, 16, 12288), bf), pltpu.VMEM((4, 80, 896), bf),
            pltpu.VMEM((16, 12288), jnp.float32), pltpu.VMEM((80, 896), jnp.float32),
            pltpu.SemaphoreType.DMA((126,)), pltpu.SemaphoreType.DMA((126,)), pltpu.SemaphoreType.DMA((4, 2)), pltpu.SemaphoreType.DMA((2,))],
        compiler_params=pltpu.CompilerParams(collective_id=1, has_side_effects=True, vmem_limit_bytes=50 * 2**20),
        name="scatter",
    )(pd, pn)


def nn(a, b):
    return jnp.dot(a, b, preferred_element_type=F32)


def nt(a, b):
    return lax.dot_general(a, b, (((1,), (1,)), ((), ())), preferred_element_type=F32)


def tn(a, b):
    return lax.dot_general(a, b, (((0,), (0,)), ((), ())), preferred_element_type=F32)


def unpad(v, spread):
    hi = v.astype(BF)
    lo = (v - hi.astype(F32)).astype(BF)
    return nt(hi, spread) + nt(lo, spread)


def rms(v):
    return lax.rsqrt(jnp.mean(v * v, axis=-1, keepdims=True) + EPS)


def rms_back(g_normed, v, gain):
    r = rms(v)
    n = v * r
    gg = g_normed * gain
    pulled = r * (gg - n * jnp.mean(gg * n, axis=-1, keepdims=True))
    return pulled, jnp.sum(g_normed * n, axis=0, keepdims=True)


def swap(u):
    width = u.shape[1]
    lane = lax.broadcasted_iota(jnp.int32, u.shape, 1)
    return jnp.where(lane % 64 < 32, pltpu.roll(u, width - 32, 1), pltpu.roll(u, 32, 1))


def wide(table, n):
    return jnp.concatenate([table] * n, axis=1)


def variants(kv):
    kv = kv.astype(F32)
    lo = lax.broadcasted_iota(jnp.int32, kv.shape, 1) < 64
    turned = pltpu.roll(kv, 64, 1)
    return [
        jnp.where(lo, kv, 0.0).astype(BF),
        jnp.where(lo, 0.0, turned).astype(BF),
        jnp.where(lo, turned, 0.0).astype(BF),
        jnp.where(lo, 0.0, kv).astype(BF),
    ]


GROUPS = ((0, 0, (0, 1, 2, 3)), (0, 1, (0, 1, 2)), (1, 0, (4, 5, 6)), (1, 1, (3, 4, 5, 6)))


def pairs(v, which):
    return jnp.concatenate([v[:, 128 * p : 128 * p + 128] for p in which], axis=0)


def allowed_mask(ids_own, ids_all, me):
    row = me * ROWS + lax.broadcasted_iota(jnp.int32, (ROWS, 4 * ROWS), 0)
    col = lax.broadcasted_iota(jnp.int32, (ROWS, 4 * ROWS), 1)
    return (ids_own == ids_all) & (col <= row)


def probs(q, k_var, mask, which):
    s = nt(pairs(q, which), k_var).reshape(len(which), ROWS, 4 * ROWS)
    s = jnp.where(mask[None], s, -1e9)
    e = jnp.exp(s - jnp.max(s, axis=-1, keepdims=True))
    p = e / jnp.sum(e, axis=-1, keepdims=True)
    return p.reshape(len(which) * ROWS, 4 * ROWS)


def greet(peers):
    barrier = pltpu.get_barrier_semaphore()
    for c in peers:
        pl.semaphore_signal(barrier, inc=1, device_id={"ctx": c}, device_id_type=MESH)
    pl.semaphore_wait(barrier, 3)


def attn_fwd_kernel(h, gain, bias, cos, sin, ids_own, ids_all, spread, gd, mid, a_out, q_out, kv_out, o_out,
                    wqkv, wout, kv, wsem, send, recv):
    me = lax.axis_index("ctx")
    peers = [lax.rem(me + d, 4) for d in (1, 2, 3)]
    loads = [pltpu.make_async_copy(gd.at[:, pl.ds(0, QKV)], wqkv, wsem.at[0]),
             pltpu.make_async_copy(gd.at[:, pl.ds(QKV, D)], wout, wsem.at[1])]
    for c in loads:
        c.start()
    greet(peers)
    x = h[...]
    a = (x * rms(x) * gain[...]).astype(BF)
    a = nn(a, spread[...]).astype(BF)
    a_out[...] = a
    loads[0].wait()
    lin = nn(a, wqkv[...]) + bias[...]
    qk = lin[:, :1024]
    qk = qk * wide(cos[...], 8) + swap(qk) * wide(sin[...], 8)
    q = (qk[:, :D] * HEAD**-0.5).astype(BF)
    q_out[...] = q
    kv[me] = jnp.concatenate([qk[:, D:], lin[:, 1024:]], axis=1).astype(BF)
    moves = [pltpu.make_async_remote_copy(src_ref=kv.at[me], dst_ref=kv.at[me], send_sem=send.at[d], recv_sem=recv.at[d],
                                          device_id={"ctx": c}, device_id_type=MESH) for d, c in enumerate(peers)]
    for m in moves:
        m.start()
    mask = allowed_mask(ids_own[...], ids_all[...], me)
    for m in moves:
        m.wait_recv()
    for m in moves:
        m.wait_send()
    full = kv[...].reshape(4 * ROWS, 256)
    kv_out[...] = full
    ks, vs = variants(full[:, :128]), variants(full[:, 128:])
    o = [jnp.zeros((ROWS, 128), F32)] * 7
    for g, par, which in GROUPS:
        p = probs(q, ks[2 * g + par], mask, which).astype(BF)
        part = nn(p, vs[2 * g + par])
        for i, w in enumerate(which):
            o[w] = o[w] + part[i * ROWS : (i + 1) * ROWS]
    o = nn(jnp.concatenate(o, axis=1).astype(BF), spread[...]).astype(BF)
    o_out[...] = o
    loads[1].wait()
    mid[...] = x + nn(o, wout[...])


def attn_fwd(h, gain, bias, cos, sin, ids_own, ids_all, spread, gd):
    sds = jax.ShapeDtypeStruct
    return pl.pallas_call(
        attn_fwd_kernel,
        out_shape=(sds((ROWS, D), F32), sds((ROWS, DP), BF), sds((ROWS, D), BF), sds((4 * ROWS, 256), BF), sds((ROWS, DP), BF)),
        in_specs=[VM] * 8 + [ANY],
        out_specs=(VM,) * 5,
        scratch_shapes=[pltpu.VMEM((DP, QKV), BF), pltpu.VMEM((DP, D), BF), pltpu.VMEM((4, ROWS, 256), BF),
                        pltpu.SemaphoreType.DMA((2,)), pltpu.SemaphoreType.DMA((3,)), pltpu.SemaphoreType.DMA((3,))],
        compiler_params=pltpu.CompilerParams(collective_id=2, has_side_effects=True, vmem_limit_bytes=48 * 2**20),
        name="attn_fwd",
    )(h, gain, bias, cos, sin, ids_own, ids_all, spread, gd)


def attn_bwd_kernel(gmid, h, q_ref, kv_ref, gain, cos, sin, ids_own, ids_all, spread, gd,
                    gh, gh_low, glin_out, gz_out, ggain, gbias, wqkv, wout, part, got, wsem, send, recv):
    me = lax.axis_index("ctx")
    peers = [lax.rem(me + d, 4) for d in (1, 2, 3)]
    loads = [pltpu.make_async_copy(gd.at[:, pl.ds(0, QKV)], wqkv, wsem.at[0]),
             pltpu.make_async_copy(gd.at[:, pl.ds(QKV, D)], wout, wsem.at[1])]
    for c in loads:
        c.start()
    greet(peers)
    gm = gmid[...]
    gz = gm.astype(BF)
    gz_out[...] = gz
    loads[1].wait()
    go = nt(nt(gz, wout[...]).astype(BF), spread[...]).astype(BF)
    q = q_ref[...]
    full = kv_ref[...]
    ks, vs = variants(full[:, :128]), variants(full[:, 128:])
    mask = allowed_mask(ids_own[...], ids_all[...], me)
    gq = [jnp.zeros((ROWS, 128), F32)] * 7
    gk, gv = [], []
    for g, par, which in GROUPS:
        p = probs(q, ks[2 * g + par], mask, which)
        go_here = pairs(go, which)
        gp = nt(go_here, vs[2 * g + par])
        gv.append(tn(p.astype(BF), go_here))
        gs = (p * (gp - jnp.sum(p * gp, axis=-1, keepdims=True))).astype(BF)
        gk.append(tn(gs, pairs(q, which)))
        back = nn(gs, ks[2 * g + par])
        for i, w in enumerate(which):
            gq[w] = gq[w] + back[i * ROWS : (i + 1) * ROWS]
    lo = lax.broadcasted_iota(jnp.int32, (4 * ROWS, 128), 1) < 64

    def merged(e0, o0, e1, o1):
        return jnp.where(lo, e0, o1) + pltpu.roll(jnp.where(lo, e1, o0), 64, 1)

    part[...] = jnp.concatenate([merged(*gk), merged(*gv)], axis=1).reshape(4, ROWS, 256)
    moves = [pltpu.make_async_remote_copy(src_ref=part.at[c], dst_ref=got.at[d], send_sem=send.at[d], recv_sem=recv.at[d],
                                          device_id={"ctx": c}, device_id_type=MESH) for d, c in enumerate(peers)]
    for m in moves:
        m.start()
    cs, sn = cos[...], sin[...]
    gq = jnp.concatenate(gq, axis=1) * HEAD**-0.5
    gq = gq * wide(cs, 7) + swap(gq * wide(sn, 7))
    for m in moves:
        m.wait_recv()
    for m in moves:
        m.wait_send()
    own = part[me] + got[0] + got[1] + got[2]
    gk = own[:, :128]
    gk = gk * cs + swap(gk * sn)
    glin = jnp.concatenate([gq, gk, own[:, 128:]], axis=1).astype(BF)
    glin_out[...] = glin
    gbias[...] = jnp.sum(glin.astype(F32), axis=0, keepdims=True)
    loads[0].wait()
    ga = unpad(nt(glin, wqkv[...]), spread[...])
    pulled, gg = rms_back(ga, h[...], gain[...])
    ggain[...] = gg
    gh[...] = gm + pulled
    gh_low[...] = (gm + pulled).astype(BF)


def attn_bwd(gmid, h, q, kv, gain, cos, sin, ids_own, ids_all, spread, gd):
    sds = jax.ShapeDtypeStruct
    return pl.pallas_call(
        attn_bwd_kernel,
        out_shape=(sds((ROWS, D), F32), sds((ROWS, D), BF), sds((ROWS, QKV), BF), sds((ROWS, D), BF), sds((1, D), F32), sds((1, QKV), F32)),
        in_specs=[VM] * 10 + [ANY],
        out_specs=(VM,) * 6,
        scratch_shapes=[pltpu.VMEM((DP, QKV), BF), pltpu.VMEM((DP, D), BF), pltpu.VMEM((4, ROWS, 256), F32), pltpu.VMEM((3, ROWS, 256), F32),
                        pltpu.SemaphoreType.DMA((2,)), pltpu.SemaphoreType.DMA((3,)), pltpu.SemaphoreType.DMA((3,))],
        compiler_params=pltpu.CompilerParams(collective_id=3, has_side_effects=True, vmem_limit_bytes=48 * 2**20),
        name="attn_bwd",
    )(gmid, h, q, kv, gain, cos, sin, ids_own, ids_all, spread, gd)


def ffn_fwd_kernel(mid, gain, spread, wg, wu, wd, y, y_low, b_out, gate, up, m_out, acc):
    i = pl.program_id(0)

    @pl.when(i == 0)
    def _():
        v = mid[...]
        b_out[...] = nn((v * rms(v) * gain[...]).astype(BF), spread[...]).astype(BF)
        acc[...] = v

    b = b_out[...]
    gt, u = nn(b, wg[...]), nn(b, wu[...])
    gate[...] = gt.astype(BF)
    up[...] = u.astype(BF)
    m = (gt * jax.nn.sigmoid(gt) * u).astype(BF)
    m_out[...] = m
    acc[...] += nn(m, wd[...])

    @pl.when(i == pl.num_programs(0) - 1)
    def _():
        y[...] = acc[...]
        y_low[...] = acc[...].astype(BF)


def whole(shape):
    return pl.BlockSpec(shape, lambda i: (0, 0))


def ffn_fwd(mid, gain, spread, gd, gn):
    sds = jax.ShapeDtypeStruct
    steps = FP // TILE
    first = GATE // TILE
    cols = pl.BlockSpec((ROWS, TILE), lambda i: (0, i))
    return pl.pallas_call(
        ffn_fwd_kernel,
        grid=(steps,),
        out_shape=(sds((ROWS, D), F32), sds((ROWS, D), BF), sds((ROWS, DP), BF), sds((ROWS, FP), BF), sds((ROWS, FP), BF), sds((ROWS, FP), BF)),
        in_specs=[whole((ROWS, D)), whole((1, D)), whole((D, DP)),
                  pl.BlockSpec((DP, TILE), lambda i: (0, first + i)),
                  pl.BlockSpec((DP, TILE), lambda i: (0, first + steps + i)),
                  pl.BlockSpec((TILE, D), lambda i: (i, 0))],
        out_specs=(whole((ROWS, D)), whole((ROWS, D)), whole((ROWS, DP)), cols, cols, cols),
        scratch_shapes=[pltpu.VMEM((ROWS, D), F32)],
        compiler_params=pltpu.CompilerParams(vmem_limit_bytes=48 * 2**20),
        name="ffn_fwd",
    )(mid, gain, spread, gd, gd, gn)


def ffn_bwd_kernel(gy, mid, gain, spread, gate, up, wg, wu, wd, gmid, ggain, ggate, gup, acc):
    i = pl.program_id(0)

    @pl.when(i == 0)
    def _():
        acc[...] = jnp.zeros_like(acc)

    gm = nt(gy[...], wd[...])
    gt, u = gate[...].astype(F32), up[...].astype(F32)
    sg = jax.nn.sigmoid(gt)
    ggt = (gm * u * sg * (1.0 + gt * (1.0 - sg))).astype(BF)
    gu = (gm * gt * sg).astype(BF)
    ggate[...] = ggt
    gup[...] = gu
    acc[...] += nt(ggt, wg[...]) + nt(gu, wu[...])

    @pl.when(i == pl.num_programs(0) - 1)
    def _():
        pulled, gg = rms_back(unpad(acc[...], spread[...]), mid[...], gain[...])
        gmid[...] = gy[...].astype(F32) + pulled
        ggain[...] = gg


def ffn_bwd(gy, mid, gain, spread, gate, up, gd, gn):
    sds = jax.ShapeDtypeStruct
    steps = FP // TILE
    first = GATE // TILE
    cols = pl.BlockSpec((ROWS, TILE), lambda i: (0, i))
    return pl.pallas_call(
        ffn_bwd_kernel,
        grid=(steps,),
        out_shape=(sds((ROWS, D), F32), sds((1, D), F32), sds((ROWS, FP), BF), sds((ROWS, FP), BF)),
        in_specs=[whole((ROWS, D)), whole((ROWS, D)), whole((1, D)), whole((D, DP)), cols, cols,
                  pl.BlockSpec((DP, TILE), lambda i: (0, first + i)),
                  pl.BlockSpec((DP, TILE), lambda i: (0, first + steps + i)),
                  pl.BlockSpec((TILE, D), lambda i: (i, 0))],
        out_specs=(whole((ROWS, D)), whole((1, D)), cols, cols),
        scratch_shapes=[pltpu.VMEM((ROWS, DP), F32)],
        compiler_params=pltpu.CompilerParams(vmem_limit_bytes=48 * 2**20),
        name="ffn_bwd",
    )(gy, mid, gain, spread, gate, up, gd, gd, gn)


def wgrad_kernel(a, o, b, r, out):
    i = pl.program_id(0)

    @pl.when(i < 2)
    def _():
        out[...] = tn(a[...], r[...]).astype(BF)

    @pl.when(i == 2)
    def _():
        out[:, :128] = tn(a[...], r[:, :128]).astype(BF)
        out[:, 128:] = tn(o[...], r[:, 128:]).astype(BF)

    @pl.when(i == 3)
    def _():
        out[...] = tn(o[...], r[...]).astype(BF)

    @pl.when(i > 3)
    def _():
        out[...] = tn(b[...], r[...]).astype(BF)


def wgrad(a, o, b, r):
    tok = a.shape[0]
    return pl.pallas_call(
        wgrad_kernel,
        grid=(WIDE // TILE,),
        out_shape=jax.ShapeDtypeStruct((DP, WIDE), BF),
        in_specs=[whole((tok, DP))] * 3 + [pl.BlockSpec((tok, TILE), lambda i: (0, i))],
        out_specs=pl.BlockSpec((DP, TILE), lambda i: (0, i)),
        compiler_params=pltpu.CompilerParams(vmem_limit_bytes=48 * 2**20),
        name="wgrad",
    )(a, o, b, r)


def wgrad_down_kernel(m, gy, out):
    out[...] = tn(m[...], gy[...]).astype(BF)


def wgrad_down(m, gy):
    tok = m.shape[0]
    return pl.pallas_call(
        wgrad_down_kernel,
        grid=(FP // TILE,),
        out_shape=jax.ShapeDtypeStruct((FP, D), BF),
        in_specs=[pl.BlockSpec((tok, TILE), lambda i: (0, i)), whole((tok, D))],
        out_specs=pl.BlockSpec((TILE, D), lambda i: (i, 0)),
        compiler_params=pltpu.CompilerParams(vmem_limit_bytes=48 * 2**20),
        name="wgrad_down",
    )(m, gy)


def per_device(ends_in, segment_ids, norm_gains, qkv_weight, qkv_bias, out_weight, in_weight, down_weight):
    section = lax.axis_index("section")
    me = lax.axis_index("ctx")
    lead = in_weight[0].reshape(14, 2, 64, 76)
    lead = jnp.pad(lead, ((0, 0), (0, 0), (0, 0), (0, 4))).reshape(14, 2 * FP)
    rows = jnp.concatenate([qkv_weight[0], out_weight[0], lead], axis=1)
    pad = lambda v, n: jnp.pad(v, (0, n - v.shape[0]))
    extra = jnp.concatenate([pad(norm_gains[0, 0], 128), pad(norm_gains[0, 1], 128), pad(qkv_bias[0], WIDE - 256)])
    wd = jnp.concatenate([rows, extra[None], jnp.zeros((1, WIDE), BF)], axis=0)
    wn = jnp.pad(down_weight[0], ((0, 4), (0, 0)))
    gd, gn = gather(wd, wn)
    gains = [gd[:, 14, 128 * i : 128 * i + 14].reshape(1, D).astype(F32) for i in (0, 1)]
    bias = gd[:, 14, 256:274].reshape(1, QKV).astype(F32)
    gd, gn = gd.reshape(DP, WIDE), gn.reshape(FP, D)
    src = jnp.arange(D)
    spread = ((src + 2 * (src // 14))[:, None] == jnp.arange(DP)[None, :]).astype(BF)

    ids = lax.all_gather(segment_ids[:, 0], "ctx", axis=1, tiled=True)
    at = jnp.arange(4 * ROWS, dtype=jnp.int32)
    own_at = me * ROWS + at[:ROWS]
    same = (segment_ids[:, 0, :, None] == ids[:, None, :]) & (at[None, None, :] <= own_at[None, :, None])
    pos = (jnp.sum(same.astype(jnp.int32), axis=2) - 1).astype(F32)
    freq = 1000000.0 ** (-jnp.arange(0, HEAD, 2, dtype=F32) / HEAD)
    angle = pos[..., None] * freq
    c, s = jnp.cos(angle), jnp.sin(angle)
    cos = jnp.concatenate([c, c, c, c], axis=-1)
    sin = jnp.concatenate([-s, s, -s, s], axis=-1)

    def slot(t):
        return jnp.clip(t - section, 0, 1)

    def of(v, i):
        return lax.dynamic_index_in_dim(v, i, 0, keepdims=False)

    def place_of(t):
        i = slot(t)
        return of(cos, i), of(sin, i), of(segment_ids[:, 0], i)[:, None], of(ids, i)[None]

    kept = []
    incoming = None
    for t in range(3):
        h = ends_in[0, min(t, 1), 0].astype(F32)
        if t:
            h = jnp.where(section == 0, h, incoming.astype(F32))
        tables = place_of(t)
        mid, a, q, kv, o = attn_fwd(h, gains[0], bias, *tables, spread, gd)
        y, y_low, b, gate, up, m = ffn_fwd(mid, gains[1], spread, gd, gn)
        if t < 2:
            incoming = lax.ppermute(y_low, "section", [(0, 1)])
        kept.append((h, mid, a, q, kv, o, y, b, gate, up, m, tables))
    back = [None] * 3
    for u in range(3):
        t = 2 - u
        h, mid, a, q, kv, o, y, b, gate, up, m, tables = kept[t]
        first = ends_in[0, max(1 - u, 0), 0]
        here = incoming if u else jnp.zeros_like(first)
        if u == 2:
            first = jnp.zeros_like(first)
        gy = jnp.where(section == 1, first, here)
        gmid, gg1, ggate, gup = ffn_bwd(gy, mid, gains[1], spread, gate, up, gd, gn)
        gh, gh_low, glin, gz, gg0, gb = attn_bwd(gmid, h, q, kv, gains[0], *tables, spread, gd)
        if u < 2:
            incoming = lax.ppermute(gh_low, "section", [(1, 0)])
        back[t] = (gh, gy, ggate, gup, glin, gz, gg0, gg1, gb)

    def both(f):
        return jnp.concatenate([f(1), jnp.where(section == 0, f(0), f(2))], axis=0)

    a, o, b, m = (both(lambda t, i=i: kept[t][i]) for i in (2, 5, 7, 10))
    r = both(lambda t: jnp.concatenate([back[t][4], back[t][5], back[t][2], back[t][3]], axis=1))
    gy = both(lambda t: back[t][1])
    pd = wgrad(a, o, b, r).reshape(64, 16, WIDE)
    pn = wgrad_down(m, gy).reshape(64, 80, D)
    gg0, gg1, gb = (back[0][i] + back[1][i] + back[2][i] for i in (6, 7, 8))
    cell = lambda v: jnp.pad(v.reshape(64, -1), ((0, 0), (0, 128 - v.shape[1] // 64)))
    small = jnp.pad(jnp.concatenate([cell(gg0), cell(gg1), cell(gb)], axis=1), ((0, 0), (0, D - 384)))
    pn = lax.dynamic_update_slice(pn, small.astype(BF)[:, None], (0, 76, 0))
    sd, sn = scatter(pd, pn)
    ends = jnp.stack([jnp.where(section == 0, back[i][0], kept[i + 1][6]) for i in (0, 1)])
    g_in = sd[:14, GATE:].reshape(14, 2, 64, 80)[..., :76].reshape(14, 2 * FF)
    return (
        ends[None, :, None],
        jnp.stack([sn[76, :14], sn[76, 128:142]])[None],
        sd[None, :14, :QKV],
        sn[None, 76, 256:274],
        sd[None, :14, QKV:GATE],
        g_in[None],
        sn[None, :76],
    )


def solution(mesh):
    both = ("dp", "ctx")
    ends = P("section", None, "dp", "ctx", None)
    weights = (P("section", None, both), P("section", both, None), P("section", both), P("section", both, None),
               P("section", both, None), P("section", both, None))
    return jax.shard_map(per_device, mesh=mesh, in_specs=(ends, P(None, "dp", "ctx")) + weights,
                         out_specs=(ends,) + weights, check_vma=False)
```

time: 2360 us -> 573 us (0.24)
  blocking collectives: 1390 us -> 7.19 us
  Pallas kernels: 0 us -> 439 us
  waiting for transfers between devices: 271 us -> 21 us
  local copies, waits for them, and re-layouts: 290 us -> 44.2 us
  matrix products: 136 us -> 0 us
  starting transfers between devices: 125 us -> 11.7 us
  other arithmetic: 120 us -> 37.1 us
    unnamed x3 -> x0, blocking collectives: 1040 us -> none
    pallas_call x0 -> x16, Pallas kernels: none -> 439 us  [the longest x1 111 us: scatter(): pl.pallas_call(scatter_kernel, out_shape=(jax.ShapeDtypeStruct(pd.shape[1...]
    all_gather x15 -> x1, blocking collectives: 347 us -> 7.19 us  [per_device(): ids = lax.all_gather(segment_ids[:, 0], 'ctx', axis=1, tiled=True)]
    dot_general x34 -> x0, matrix products: 136 us -> none  [the longest x4 34.6 us: contract_rows(): lax.dot_general(left_flat, right_flat, (((0,), (0,)), ((), ())), preferre...]
    reduce_scatter x6 -> x0, waiting for transfers between devices: 122 us -> none  [the longest x3 72.2 us: per_device(): lax.psum_scatter(grad_values, 'ctx', scatter_dimension=1, tiled=True)]
    unnamed x28 -> x0, starting transfers between devices: 119 us -> none
    unnamed x224 -> x186, local copies, waits for them, and re-layouts: 140 us -> 26.9 us
    all_gather x4 -> x0, waiting for transfers between devices: 95.9 us -> none  [the longest x1 95.8 us: per_device(): lax.all_gather(in_weight[0], ('dp', 'ctx'), axis=0, tiled=True)]
  transfers between devices with their start and end apart: 42 -> 4, of which waited for: 13 -> 4; matrix products, arithmetic and copies ran while one was open for 41% -> 1% of each run, Pallas kernels for 0% -> 0%
where the time goes in v1:
time: 573 us; the launch traced here: 562 us
  Pallas kernels  439 us (77%)
  local copies, waits for them, and re-layouts  44.2 us (8%)
  other arithmetic  37.1 us (6%)
  waiting for transfers between devices  21 us (4%)
  starting transfers between devices  11.7 us (2%)
  blocking collectives  7.19 us (1%)
    pallas_call x1, Pallas kernels, scatter(): pl.pallas_call(scatter_kernel, out_shape=(jax.ShapeDtypeStruct(pd.shape[1...  111 us
    pallas_call x1, Pallas kernels, gather(): pl.pallas_call(gather_kernel, out_shape=(jax.ShapeDtypeStruct((64,) + wd....  101 us
    pallas_call x3, Pallas kernels, ffn_bwd(): pl.pallas_call(ffn_bwd_kernel, grid=(steps,), out_shape=(sds((ROWS, D), F...  59.9 us
    pallas_call x3, Pallas kernels, attn_bwd(): pl.pallas_call(attn_bwd_kernel, out_shape=(sds((ROWS, D), F32), sds((ROWS...  53.2 us
    pallas_call x3, Pallas kernels, ffn_fwd(): pl.pallas_call(ffn_fwd_kernel, grid=(steps,), out_shape=(sds((ROWS, D), F...  50.4 us
    pallas_call x3, Pallas kernels, attn_fwd(): pl.pallas_call(attn_fwd_kernel, out_shape=(sds((ROWS, D), F32), sds((ROWS...  33 us
    unnamed x186, local copies, waits for them, and re-layouts  26.9 us
    pallas_call x1, Pallas kernels, wgrad(): pl.pallas_call(wgrad_kernel, grid=(WIDE // TILE,), out_shape=jax.ShapeDty...  22.7 us
  transfers between devices with their start and end apart: 4, of which 4 were waited for; matrix products, arithmetic and copies ran while one was open for 1% of the time, Pallas kernels for 0%

profile of v1, /device:TPU:2, one launch (start us, length us, event | category | flops | bytes accessed | tf_op | source)
XLA Modules:
  0.0 562.2 jit_solution(15784184913326695114)
XLA Ops:
  0.7 7.2 %all-gather = s32[2,1,512]{2,1,0:T(1,128)S(1)} all-gather(s32[2,1,128]{2,1,0:T(1,128)} %param.9), channel_id=2, replica_groups=mesh['section'=2,'dp'=16,'ctx'=4] {'ctx'}, dimensions={2}, use_global_device_ids=true | all-gather | bytes 5120 | tf_op jit(solution)/shard_map/all_gather | solution.py:699
  10.1 2.5 reshape_squeeze.2
  12.5 1.6 pad.42.wn
  15.2 1.7 maximum_maximum_fusion.wd
  16.8 101.1 %gather.1 = (bf16[64,16,12288]{2,1,0:T(8,128)(2,1)}, bf16[64,80,896]{2,1,0:T(8,128)(2,1)}) custom-call(bf16[16,12288]{1,0:T(8,128)(2,1)} %maximum_maximum_fusion.wd, bf16[80,896]{1,0:T(8,128)(2,1)} %pad.42.wn), custom_call_target="tpu_custom_call" | custom-call | tf_op jit(solution)/shard_map/gather/pallas_call | solution.py:149
  117.9 1.0 convert_reduce_fusion.2
  118.9 1.2 convert_reduce_fusion.1
  122.5 11.1 %attn_fwd.3 = (f32[128,896]{1,0:T(8,128)S(1)}, bf16[128,1024]{1,0:T(8,128)(2,1)S(1)}, bf16[128,896]{1,0:T(8,128)(2,1)S(1)}, bf16[512,256]{1,0:T(8,128)(2,1)S(1)}, bf16[128,1024]{1,0:T(8,128)(2,1)S(1)}) custom-call(f32[128,896]{1,0:T(8,128)S(1)} %get-tuple-element.158.h, f32[1,896]{1,0:T(1,128)S(1)} %reshape.161.gain, f32[1,1152]{1,0:T(1,128)S(1)} %reshape.162.bias, ...), custom_call_target="tpu_custom_call" | custom-call | tf_op jit(solution)/shard_map/attn_fwd/pallas_call | solution.py:454
  136.4 17.0 %ffn_fwd.3 = (f32[128,896]{1,0:T(8,128)}, bf16[128,896]{1,0:T(8,128)(2,1)}, bf16[128,1024]{1,0:T(8,128)(2,1)S(1)}, bf16[128,5120]{1,0:T(8,128)(2,1)S(1)}, bf16[1...) custom-call(f32[128,896]{1,0:T(8,128)S(1)} %get-tuple-element.71.mid, f32[1,896]{1,0:T(1,128)S(1)} %reshape.163.gain, ...), custom_call_target="tpu_custom_call" | custom-call | tf_op jit(solution)/shard_map/ffn_fwd/pallas_call | solution.py:573
  153.4 1.1 copy-done.25
  154.6 1.1 copy-done.27
  155.6 1.0 copy-done.29
  157.4 3.8 collective-permute-start
  161.3 5.1 collective-permute-done
  166.4 1.1 convert_select_fusion.1.h
  167.5 10.9 %attn_fwd.4 = (f32[128,896]{1,0:T(8,128)S(1)}, bf16[128,1024]{1,0:T(8,128)(2,1)S(1)}, bf16[128,896]{1,0:T(8,128)(2,1)S(1)}, bf16[512,256]{1,0:T(8,128)(2,1)S(1)}, bf16[128,1024]{1,0:T(8,128)(2,1)S(1)}) custom-call(f32[128,896]{1,0:T(8,128)S(1)} %convert_select_fusion.1.h, f32[1,896]{1,0:T(1,128)S(1)} %reshape.161.gain, f32[1,1152]{1,0:T(1,128)S(1)} %reshape.162.bias, ...), custom_call_target="tpu_custom_call" | custom-call | tf_op jit(solution)/shard_map/attn_fwd/pallas_call | solution.py:454
  181.3 16.3 %ffn_fwd.4 = (f32[128,896]{1,0:T(8,128)S(1)}, bf16[128,896]{1,0:T(8,128)(2,1)S(1)}, bf16[128,1024]{1,0:T(8,128)(2,1)S(1)}, bf16[128,5120]{1,0:T(8,128)(2,1)S(1)}...) custom-call(f32[128,896]{1,0:T(8,128)S(1)} %get-tuple-element.74.mid, f32[1,896]{1,0:T(1,128)S(1)} %reshape.163.gain, ...), custom_call_target="tpu_custom_call" | custom-call | tf_op jit(solution)/shard_map/ffn_fwd/pallas_call | solution.py:573
  197.6 1.1 copy-done.21
  198.6 1.0 copy-done.30
  199.7 1.1 copy-done.32
  202.2 5.1 collective-permute-start.1
  207.4 5.0 collective-permute-done.1
  212.3 1.1 convert_select_fusion.h
  213.5 10.9 %attn_fwd.5 = (f32[128,896]{1,0:T(8,128)S(1)}, bf16[128,1024]{1,0:T(8,128)(2,1)S(1)}, bf16[128,896]{1,0:T(8,128)(2,1)S(1)}, bf16[512,256]{1,0:T(8,128)(2,1)S(1)}, bf16[128,1024]{1,0:T(8,128)(2,1)S(1)}) custom-call(f32[128,896]{1,0:T(8,128)S(1)} %convert_select_fusion.h, f32[1,896]{1,0:T(1,128)S(1)} %reshape.161.gain, f32[1,1152]{1,0:T(1,128)S(1)} %reshape.162.bias, ...), custom_call_target="tpu_custom_call" | custom-call | tf_op jit(solution)/shard_map/attn_fwd/pallas_call | solution.py:454
  224.4 17.1 %ffn_fwd.5 = (f32[128,896]{1,0:T(8,128)S(1)}, bf16[128,896]{1,0:T(8,128)(2,1)}, bf16[128,1024]{1,0:T(8,128)(2,1)S(1)}, bf16[128,5120]{1,0:T(8,128)(2,1)S(1)}, bf...) custom-call(f32[128,896]{1,0:T(8,128)S(1)} %get-tuple-element.76.mid, f32[1,896]{1,0:T(1,128)S(1)} %reshape.163.gain, ...), custom_call_target="tpu_custom_call" | custom-call | tf_op jit(solution)/shard_map/ffn_fwd/pallas_call | solution.py:573
  241.5 1.1 copy-done.33
  242.6 19.5 %ffn_bwd.3 = (f32[128,896]{1,0:T(8,128)S(1)}, f32[1,896]{1,0:T(1,128)S(1)}, bf16[128,5120]{1,0:T(8,128)(2,1)S(1)}, bf16[128,5120]{1,0:T(8,128)(2,1)S(1)}) custom-call(bf16[128,896]{1,0:T(8,128)(2,1)S(1)} %get-tuple-element.159.gy, f32[128,896]{1,0:T(8,128)S(1)} %get-tuple-element.76.mid, f32[1,896]{1,0:T(1,128)S(1)} %reshape.163.gain, ...), custom_call_target="tpu_custom_call" | custom-call | tf_op jit(solution)/shard_map/ffn_bwd/pallas_call | solution.py:616
  262.1 1.1 copy-done.16
  263.2 17.9 %attn_bwd.3 = (f32[128,896]{1,0:T(8,128)}, bf16[128,896]{1,0:T(8,128)(2,1)S(1)}, bf16[128,1152]{1,0:T(8,128)(2,1)S(1)}, bf16[128,896]{1,0:T(8,128)(2,1)S(1)}, f3...) custom-call(f32[128,896]{1,0:T(8,128)S(1)} %get-tuple-element.79.gmid, f32[128,896]{1,0:T(8,128)S(1)} %convert_select_fusion.h, ...), custom_call_target="tpu_custom_call" | custom-call | tf_op jit(solution)/shard_map/attn_bwd/pallas_call | solution.py:529
  281.2 1.4 collective-permute-start.2
  286.6 3.6 collective-permute-done.2
  290.3 20.2 %ffn_bwd.4 = (f32[128,896]{1,0:T(8,128)S(1)}, f32[1,896]{1,0:T(1,128)S(1)}, bf16[128,5120]{1,0:T(8,128)(2,1)S(1)}, bf16[128,5120]{1,0:T(8,128)(2,1)S(1)}) custom-call(bf16[128,896]{1,0:T(8,128)(2,1)S(1)} %bitcast_select_fusion.gy, f32[128,896]{1,0:T(8,128)S(1)} %copy-done.14, f32[1,896]{1,0:T(1,128)S(1)} %reshape.163.gain, bf16[896,1024]{1,0:T(8,128)(2,1)} %copy-done, ...), custom_call_target="tpu_custom_call" | custom-call | tf_op jit(solution)/shard_map/ffn_bwd/pallas_call | solution.py:616
  310.5 1.1 copy-done.17
  312.3 17.5 %attn_bwd.4 = (f32[128,896]{1,0:T(8,128)S(1)}, bf16[128,896]{1,0:T(8,128)(2,1)S(1)}, bf16[128,1152]{1,0:T(8,128)(2,1)S(1)}, bf16[128,896]{1,0:T(8,128)(2,1)S(1)}...) custom-call(f32[128,896]{1,0:T(8,128)S(1)} %get-tuple-element.85.gmid, f32[128,896]{1,0:T(8,128)S(1)} %convert_select_fusion.1.h, ...), custom_call_target="tpu_custom_call" | custom-call | tf_op jit(solution)/shard_map/attn_bwd/pallas_call | solution.py:529
  330.5 1.4 collective-permute-start.3
  332.8 7.4 %collective-permute-done.3 = bf16[128,896]{1,0:T(8,128)(2,1)S(1)} collective-permute-done((bf16[128,896]{1,0:T(8,128)(2,1)S(1)}, bf16[128,896]{1,0:T(8,128)(2,1)S(1)}, u32[]{:S(2)}, u32[]{:S(2)}) %collective-permute-start.3) | collective-permute-done | bytes 229408 | tf_op jit(solution)/shard_map/ppermute | solution.py:744
  340.3 20.2 %ffn_bwd.5 = (f32[128,896]{1,0:T(8,128)S(1)}, f32[1,896]{1,0:T(1,128)S(1)}, bf16[128,5120]{1,0:T(8,128)(2,1)S(1)}, bf16[128,5120]{1,0:T(8,128)(2,1)S(1)}) custom-call(bf16[128,896]{1,0:T(8,128)(2,1)S(1)} %get-tuple-element.157.gy, f32[128,896]{1,0:T(8,128)S(1)} %copy-done.12, f32[1,896]{1,0:T(1,128)S(1)} %reshape.163.gain, bf16[896,1024]{1,0:T(8,128)(2,1)} %copy-done, ...), custom_call_target="tpu_custom_call" | custom-call | tf_op jit(solution)/shard_map/ffn_bwd/pallas_call | solution.py:616
  360.6 1.0 copy-done.24
  362.3 17.7 %attn_bwd.5 = (f32[128,896]{1,0:T(8,128)S(1)}, bf16[128,896]{1,0:T(8,128)(2,1)}, bf16[128,1152]{1,0:T(8,128)(2,1)S(1)}, bf16[128,896]{1,0:T(8,128)(2,1)S(1)}, f3...) custom-call(f32[128,896]{1,0:T(8,128)S(1)} %get-tuple-element.91.gmid, f32[128,896]{1,0:T(8,128)S(1)} %get-tuple-element.158.h, ...), custom_call_target="tpu_custom_call" | custom-call | tf_op jit(solution)/shard_map/attn_bwd/pallas_call | solution.py:529
  385.6 7.7 %wgrad_down.1 = bf16[5120,896]{1,0:T(8,128)(2,1)} custom-call(bf16[256,5120]{1,0:T(8,128)(2,1)S(1)} %pad_maximum_fusion.1.m, bf16[256,896]{1,0:T(8,128)(2,1)S(1)} %pad_maximum_fusion.5.gy), custom_call_target="tpu_custom_call" | custom-call | tf_op jit(solution)/shard_map/wgrad_down/pallas_call | solution.py:671
  393.3 5.2 dynamic_update_slice.3.pn
  398.5 3.2 maximum_select_fusion
  402.1 18.6 %pad_maximum_fusion.r = bf16[256,12288]{1,0:T(8,128)(2,1)} fusion(bf16[128,12288]{1,0:T(8,128)(2,1)S(1)} %maximum_select_fusion, bf16[128,5120]{1,0:T(8,128)(2,1)S(1)} %copy-done.20, bf16[128,5120]{1,0:T(8,128)(2,1)S(1)} %copy-done.18, bf16[128,896]{1,0:T(8,128)(2,1)S(1)} %copy-done.73, bf16[128,1152]{1,0:T(8,128)(2,1)S(1)} %copy-done.53), kind=kLoop, calls=%fused_computation | loop fusion | flops 31457280 | bytes 12582912 | tf_op jit(solution)/shard_map/concatenate | solution.py:748
  420.7 22.7 %wgrad.1 = bf16[1024,12288]{1,0:T(8,128)(2,1)} custom-call(bf16[256,1024]{1,0:T(8,128)(2,1)S(1)} %copy-done.7, bf16[256,1024]{1,0:T(8,128)(2,1)S(1)} %copy-done.6, bf16[256,1024]{1,0:T(8,128)(2,1)S(1)} %copy-done.8, bf16[256,12288]{1,0:T(8,128)(2,1)} %pad_maximum_fusion.r), custom_call_target="tpu_custom_call" | custom-call | tf_op jit(solution)/shard_map/wgrad/pallas_call | solution.py:654
  443.4 110.8 %scatter.1 = (f32[16,12288]{1,0:T(8,128)S(1)}, f32[80,896]{1,0:T(8,128)S(1)}) custom-call(bf16[64,16,12288]{2,1,0:T(8,128)(2,1)} %bitcast.97, bf16[64,80,896]{2,1,0:T(8,128)(2,1)} %dynamic_update_slice.3.pn), custom_call_target="tpu_custom_call" | custom-call | tf_op jit(solution)/shard_map/scatter/pallas_call | solution.py:312
  554.9 1.0 copy.46
  557.7 2.4 broadcast_in_dim_reshape.3
  560.2 1.0 maximum_bitcast_fusion
  (232 shorter events, 29.2 us)
Async XLA Ops:
  0.6 119.7 %copy-start.90 = (s32[2,1,128]{2,1,0:T(1,128)S(1)}, s32[2,1,128]{2,1,0:T(1,128)}, u32[]{:S(2)}) copy-start(s32[2,1,128]{2,1,0:T(1,128)} %param.9) | copy-start | bytes 3076
  14.2 108.1 %copy-start.87 = (bf16[1,2,1,128,896]{4,3,2,1,0:T(8,128)(2,1)S(1)}, bf16[1,2,1,128,896]{4,3,2,1,0:T(8,128)(2,1)}, u32[]{:S(2)}) copy-start(bf16[1,2,1,128,896]{4,3,2,1,0:T(8,128)(2,1)} %param.8) | copy-start | bytes 1376260
  120.6 12.9 %copy-start.34 = (s32[128,1]{1,0:T(8,128)}, s32[128,1]{1,0:T(8,128)S(1)}, u32[]{:S(2)}) copy-start(s32[128,1]{1,0:T(8,128)S(1)} %copy.36.ids_own) | copy-start | bytes 1540
  121.5 12.1 %copy-start.38 = (f32[128,128]{1,0:T(8,128)}, f32[128,128]{1,0:T(8,128)S(1)}, u32[]{:S(2)}) copy-start(f32[128,128]{1,0:T(8,128)S(1)} %get-tuple-element.167.cos) | copy-start | bytes 196612
  121.5 46.0 %copy-start.42 = (f32[128,128]{1,0:T(8,128)}, f32[128,128]{1,0:T(8,128)S(1)}, u32[]{:S(2)}) copy-start(f32[128,128]{1,0:T(8,128)S(1)} %get-tuple-element.166.cos) | copy-start | bytes 196612
  121.5 12.0 %copy-start.40 = (f32[128,128]{1,0:T(8,128)}, f32[128,128]{1,0:T(8,128)S(1)}, u32[]{:S(2)}) copy-start(f32[128,128]{1,0:T(8,128)S(1)} %get-tuple-element.164.sin) | copy-start | bytes 196612
  121.6 45.9 %copy-start.44 = (f32[128,128]{1,0:T(8,128)}, f32[128,128]{1,0:T(8,128)S(1)}, u32[]{:S(2)}) copy-start(f32[128,128]{1,0:T(8,128)S(1)} %get-tuple-element.163.sin) | copy-start | bytes 196612
  121.9 11.7 %copy-start = (bf16[896,1024]{1,0:T(8,128)(2,1)}, bf16[896,1024]{1,0:T(8,128)(2,1)S(1)}, u32[]{:S(2)}) copy-start(bf16[896,1024]{1,0:T(8,128)(2,1)S(1)} %fusion.spread) | copy-start | bytes 5505028
  122.4 120.1 %copy-start.9 = (bf16[128,896]{1,0:T(8,128)(2,1)}, bf16[128,896]{1,0:T(8,128)(2,1)S(1)}, u32[]{:S(2)}) copy-start(bf16[128,896]{1,0:T(8,128)(2,1)S(1)} %get-tuple-element.159.gy) | copy-start | bytes 688132
  136.4 17.0 %copy-start.11 = (f32[128,896]{1,0:T(8,128)}, f32[128,896]{1,0:T(8,128)S(1)}, u32[]{:S(2)}) copy-start(f32[128,896]{1,0:T(8,128)S(1)} %get-tuple-element.71.mid) | copy-start | bytes 1376260
  136.4 31.1 %copy-start.1 = (bf16[896,1024]{1,0:T(8,128)(2,1)S(1)}, bf16[896,1024]{1,0:T(8,128)(2,1)}, u32[]{:S(2)}) copy-start(bf16[896,1024]{1,0:T(8,128)(2,1)} %copy-done) | copy-start | bytes 5505028
  157.4 9.0 %collective-permute-start = (bf16[128,896]{1,0:T(8,128)(2,1)}, bf16[128,896]{1,0:T(8,128)(2,1)}, u32[]{:S(2)}, u32[]{:S(2)}) collective-permute-start(bf16[128,896]{1,0:T(8,128)(2,1)} %get-tuple-element.73), channel_id=1, source_target_pairs={{0,64},{1,65},{2,66},{3,67},{4,68},{5,69},{6,70},{7,71},{8,72},{9,... | collective-permute-start | bytes 688136 | tf_op jit(solution)/shard_map/ppermute | solution.py:730
  161.3 17.2 %copy-start.36 = (s32[128,1]{1,0:T(8,128)}, s32[128,1]{1,0:T(8,128)S(1)}, u32[]{:S(2)}) copy-start(s32[128,1]{1,0:T(8,128)S(1)} %copy.37.ids_own) | copy-start | bytes 1540
  181.3 16.3 %copy-start.13 = (f32[128,896]{1,0:T(8,128)}, f32[128,896]{1,0:T(8,128)S(1)}, u32[]{:S(2)}) copy-start(f32[128,896]{1,0:T(8,128)S(1)} %get-tuple-element.74.mid) | copy-start | bytes 1376260
  181.3 32.2 %copy-start.2 = (bf16[896,1024]{1,0:T(8,128)(2,1)S(1)}, bf16[896,1024]{1,0:T(8,128)(2,1)}, u32[]{:S(2)}) copy-start(bf16[896,1024]{1,0:T(8,128)(2,1)} %copy-done) | copy-start | bytes 5505028
  202.2 10.1 %collective-permute-start.1 = (bf16[128,896]{1,0:T(8,128)(2,1)S(1)}, bf16[128,896]{1,0:T(8,128)(2,1)}, u32[]{:S(2)}, u32[]{:S(2)}) collective-permute-start(bf16[128,896]{1,0:T(8,128)(2,1)S(1)} %get-tuple-element.75), channel_id=1, source_target_pairs={{0,64},{1,65},{2,66},{3,67},{4,68},{5,69},{6,70},{7,71},{8,72},{9,... | collective-permute-start | bytes 688136 | tf_op jit(solution)/shard_map/ppermute | solution.py:730
  242.6 20.6 %copy-start.3 = (bf16[896,1024]{1,0:T(8,128)(2,1)S(1)}, bf16[896,1024]{1,0:T(8,128)(2,1)}, u32[]{:S(2)}) copy-start(bf16[896,1024]{1,0:T(8,128)(2,1)} %copy-done) | copy-start | bytes 5505028
  263.2 18.0 %copy-start.15 = (bf16[128,5120]{1,0:T(8,128)(2,1)}, bf16[128,5120]{1,0:T(8,128)(2,1)S(1)}, u32[]{:S(2)}) copy-start(bf16[128,5120]{1,0:T(8,128)(2,1)S(1)} %get-tuple-element.117) | copy-start | bytes 3932164
  263.2 18.0 %copy-start.79 = (f32[1,896]{1,0:T(1,128)}, f32[1,896]{1,0:T(1,128)S(1)}, u32[]{:S(2)}) copy-start(f32[1,896]{1,0:T(1,128)S(1)} %get-tuple-element.127) | copy-start | bytes 10756
  263.2 19.5 %copy-start.64 = (bf16[128,1024]{1,0:T(8,128)(2,1)S(1)}, bf16[128,1024]{1,0:T(8,128)(2,1)}, u32[]{:S(2)}) copy-start(bf16[128,1024]{1,0:T(8,128)(2,1)} %copy-done.63) | copy-start | bytes 786436
  263.2 19.5 %copy-start.70 = (bf16[128,1024]{1,0:T(8,128)(2,1)S(1)}, bf16[128,1024]{1,0:T(8,128)(2,1)}, u32[]{:S(2)}) copy-start(bf16[128,1024]{1,0:T(8,128)(2,1)} %copy-done.69) | copy-start | bytes 786436
  263.2 20.4 %copy-start.60 = (bf16[128,1024]{1,0:T(8,128)(2,1)S(1)}, bf16[128,1024]{1,0:T(8,128)(2,1)}, u32[]{:S(2)}) copy-start(bf16[128,1024]{1,0:T(8,128)(2,1)} %copy-done.59) | copy-start | bytes 786436
  281.2 9.0 %collective-permute-start.2 = (bf16[128,896]{1,0:T(8,128)(2,1)S(1)}, bf16[128,896]{1,0:T(8,128)(2,1)S(1)}, u32[]{:S(2)}, u32[]{:S(2)}) collective-permute-start(bf16[128,896]{1,0:T(8,128)(2,1)S(1)} %get-tuple-element.82), channel_id=1, source_target_pairs={{64,0},{65,1},{66,2},{67,3},{68,4},{69,5},{70,6},{71,7},{72,8},{73... | collective-permute-start | bytes 688136 | tf_op jit(solution)/shard_map/ppermute | solution.py:744
  290.2 22.0 %copy-start.4 = (bf16[896,1024]{1,0:T(8,128)(2,1)S(1)}, bf16[896,1024]{1,0:T(8,128)(2,1)}, u32[]{:S(2)}) copy-start(bf16[896,1024]{1,0:T(8,128)(2,1)} %copy-done) | copy-start | bytes 5505028
  290.2 22.0 %copy-start.37 = (s32[128,1]{1,0:T(8,128)S(1)}, s32[128,1]{1,0:T(8,128)}, u32[]{:S(2)}) copy-start(s32[128,1]{1,0:T(8,128)} %copy-done.36) | copy-start | bytes 1540
  290.2 22.0 %copy-start.43 = (f32[128,128]{1,0:T(8,128)S(1)}, f32[128,128]{1,0:T(8,128)}, u32[]{:S(2)}) copy-start(f32[128,128]{1,0:T(8,128)} %copy-done.42) | copy-start | bytes 196612
  290.2 22.0 %copy-start.45 = (f32[128,128]{1,0:T(8,128)S(1)}, f32[128,128]{1,0:T(8,128)}, u32[]{:S(2)}) copy-start(f32[128,128]{1,0:T(8,128)} %copy-done.44) | copy-start | bytes 196612
  290.3 22.0 %copy-start.58 = (bf16[512,256]{1,0:T(8,128)(2,1)S(1)}, bf16[512,256]{1,0:T(8,128)(2,1)}, u32[]{:S(2)}) copy-start(bf16[512,256]{1,0:T(8,128)(2,1)} %copy-done.57) | copy-start | bytes 786436
  290.3 22.0 %copy-start.78 = (bf16[128,896]{1,0:T(8,128)(2,1)S(1)}, bf16[128,896]{1,0:T(8,128)(2,1)}, u32[]{:S(2)}) copy-start(bf16[128,896]{1,0:T(8,128)(2,1)} %copy-done.77) | copy-start | bytes 688132
  312.2 17.5 %copy-start.19 = (bf16[128,5120]{1,0:T(8,128)(2,1)}, bf16[128,5120]{1,0:T(8,128)(2,1)S(1)}, u32[]{:S(2)}) copy-start(bf16[128,5120]{1,0:T(8,128)(2,1)S(1)} %get-tuple-element.110) | copy-start | bytes 3932164
  312.3 27.9 %copy-start.10 = (bf16[128,896]{1,0:T(8,128)(2,1)S(1)}, bf16[128,896]{1,0:T(8,128)(2,1)}, u32[]{:S(2)}) copy-start(bf16[128,896]{1,0:T(8,128)(2,1)} %copy-done.9) | copy-start | bytes 688132
  330.5 9.8 %copy-start.84 = (f32[1,896]{1,0:T(1,128)}, f32[1,896]{1,0:T(1,128)S(1)}, u32[]{:S(2)}) copy-start(f32[1,896]{1,0:T(1,128)S(1)} %get-tuple-element.123) | copy-start | bytes 10756
  330.5 9.8 %copy-start.12 = (f32[128,896]{1,0:T(8,128)S(1)}, f32[128,896]{1,0:T(8,128)}, u32[]{:S(2)}) copy-start(f32[128,896]{1,0:T(8,128)} %copy-done.11) | copy-start | bytes 1376260
  330.5 9.8 %copy-start.28 = (bf16[128,5120]{1,0:T(8,128)(2,1)S(1)}, bf16[128,5120]{1,0:T(8,128)(2,1)}, u32[]{:S(2)}) copy-start(bf16[128,5120]{1,0:T(8,128)(2,1)} %copy-done.27) | copy-start | bytes 3932164
  330.5 9.6 %collective-permute-start.3 = (bf16[128,896]{1,0:T(8,128)(2,1)S(1)}, bf16[128,896]{1,0:T(8,128)(2,1)S(1)}, u32[]{:S(2)}, u32[]{:S(2)}) collective-permute-start(bf16[128,896]{1,0:T(8,128)(2,1)S(1)} %get-tuple-element.88), channel_id=1, source_target_pairs={{64,0},{65,1},{66,2},{67,3},{68,4},{69,5},{70,6},{71,7},{72,8},{73... | collective-permute-start | bytes 688136 | tf_op jit(solution)/shard_map/ppermute | solution.py:744
  340.3 21.9 %copy-start.5 = (bf16[896,1024]{1,0:T(8,128)(2,1)S(1)}, bf16[896,1024]{1,0:T(8,128)(2,1)}, u32[]{:S(2)}) copy-start(bf16[896,1024]{1,0:T(8,128)(2,1)} %copy-done) | copy-start | bytes 5505028
  340.3 21.9 %copy-start.35 = (s32[128,1]{1,0:T(8,128)S(1)}, s32[128,1]{1,0:T(8,128)}, u32[]{:S(2)}) copy-start(s32[128,1]{1,0:T(8,128)} %copy-done.34) | copy-start | bytes 1540
  340.3 21.9 %copy-start.39 = (f32[128,128]{1,0:T(8,128)S(1)}, f32[128,128]{1,0:T(8,128)}, u32[]{:S(2)}) copy-start(f32[128,128]{1,0:T(8,128)} %copy-done.38) | copy-start | bytes 196612
  340.3 21.9 %copy-start.41 = (f32[128,128]{1,0:T(8,128)S(1)}, f32[128,128]{1,0:T(8,128)}, u32[]{:S(2)}) copy-start(f32[128,128]{1,0:T(8,128)} %copy-done.40) | copy-start | bytes 196612
  340.3 21.9 %copy-start.56 = (bf16[512,256]{1,0:T(8,128)(2,1)S(1)}, bf16[512,256]{1,0:T(8,128)(2,1)}, u32[]{:S(2)}) copy-start(bf16[512,256]{1,0:T(8,128)(2,1)} %copy-done.55) | copy-start | bytes 786436
  340.3 21.9 %copy-start.76 = (bf16[128,896]{1,0:T(8,128)(2,1)S(1)}, bf16[128,896]{1,0:T(8,128)(2,1)}, u32[]{:S(2)}) copy-start(bf16[128,896]{1,0:T(8,128)(2,1)} %copy-done.75) | copy-start | bytes 688132
  362.2 17.8 %copy-start.23 = (bf16[128,5120]{1,0:T(8,128)(2,1)}, bf16[128,5120]{1,0:T(8,128)(2,1)S(1)}, u32[]{:S(2)}) copy-start(bf16[128,5120]{1,0:T(8,128)(2,1)S(1)} %get-tuple-element.113) | copy-start | bytes 3932164
  362.3 20.7 %copy-start.82 = (f32[1,896]{1,0:T(1,128)S(1)}, f32[1,896]{1,0:T(1,128)}, u32[]{:S(2)}) copy-start(f32[1,896]{1,0:T(1,128)} %copy-done.81) | copy-start | bytes 10756
  362.3 21.6 %copy-start.80 = (f32[1,896]{1,0:T(1,128)S(1)}, f32[1,896]{1,0:T(1,128)}, u32[]{:S(2)}) copy-start(f32[1,896]{1,0:T(1,128)} %copy-done.79) | copy-start | bytes 10756
  385.6 12.9 %copy-start.51 = (bf16[128,1152]{1,0:T(8,128)(2,1)S(1)}, bf16[128,1152]{1,0:T(8,128)(2,1)}, u32[]{:S(2)}) copy-start(bf16[128,1152]{1,0:T(8,128)(2,1)} %copy-done.50) | copy-start | bytes 884740
  402.1 18.7 %copy-start.6 = (bf16[256,1024]{1,0:T(8,128)(2,1)S(1)}, bf16[256,1024]{1,0:T(8,128)(2,1)}, u32[]{:S(2)}) copy-start(bf16[256,1024]{1,0:T(8,128)(2,1)} %pad_maximum_fusion.3.o) | copy-start | bytes 1572868
  402.1 18.7 %copy-start.7 = (bf16[256,1024]{1,0:T(8,128)(2,1)S(1)}, bf16[256,1024]{1,0:T(8,128)(2,1)}, u32[]{:S(2)}) copy-start(bf16[256,1024]{1,0:T(8,128)(2,1)} %pad_maximum_fusion.2.a) | copy-start | bytes 1572868
  402.1 18.7 %copy-start.8 = (bf16[256,1024]{1,0:T(8,128)(2,1)S(1)}, bf16[256,1024]{1,0:T(8,128)(2,1)}, u32[]{:S(2)}) copy-start(bf16[256,1024]{1,0:T(8,128)(2,1)} %pad_maximum_fusion.4.b) | copy-start | bytes 1572868
  (47 other events, 97.3 us)
